TPU v7x, 128 devices: a whole 4x4x4 slice. The times are simulated.
128 devices in a mesh: row: 16 (over z, y), col: 8 (over x, core).
Axes of the slice: x: 4, y: 4, z: 4, core: 2. Of those that a mesh axis runs over, the one named last changes fastest.
Arguments:
- tokens: bfloat16 [1024, 8192], P('row', 'col'), may hold values from -6 to 6
- cotangent: bfloat16 [1024, 8192], P('row', 'col'), may hold values from -3 to 3
- gate_weight: bfloat16 [8192, 14336], P('col', 'row'), may hold values from -0.0625 to 0.0625
- up_weight: bfloat16 [8192, 14336], P('col', 'row'), may hold values from -0.0625 to 0.0625
- down_weight: bfloat16 [14336, 8192], P('row', 'col'), may hold values from -0.046875 to 0.046875
- gate_mask: int32 [64, 112], P('col', 'row'), may hold values from 0 to 1
- up_mask: int32 [64, 112], P('col', 'row'), may hold values from 0 to 1
- down_mask: int32 [112, 64], P('row', 'col'), may hold values from 0 to 1
Outputs:
- output: bfloat16 [1024, 8192], P('row', 'col')
- grad_tokens: bfloat16 [1024, 8192], P('row', 'col')
- grad_gate_weight: bfloat16 [8192, 14336], P('col', 'row')
- grad_up_weight: bfloat16 [8192, 14336], P('col', 'row')
- grad_down_weight: bfloat16 [14336, 8192], P('row', 'col')
All inputs are finite; a program needn't handle non-finite values.
Results may differ from a plain program's by a relative error of at most 0.005.
Values may be sent and summed in bfloat16 or wider, within the bound.
A program may use at most 128 MiB of HBM per device.

v0:
```python
import jax
import jax.numpy as jnp
from jax import lax
from jax.sharding import PartitionSpec as P


def apply_blocks(weight, keep_mask):
    row_blocks, col_blocks = keep_mask.shape
    height = weight.shape[0] // row_blocks
    breadth = weight.shape[1] // col_blocks
    shaped = weight.reshape(row_blocks, height, col_blocks, breadth)
    return (shaped * keep_mask.astype(weight.dtype)[:, None, :, None]).reshape(weight.shape)


def column_share(values):
    return lax.psum_scatter(values, "col", scatter_dimension=1, tiled=True)


def column_rows(values):
    return lax.all_gather(values, "col", axis=1, tiled=True)


def feature_share(values):
    return lax.psum_scatter(values, "row", scatter_dimension=0, tiled=True)


def gate_grads(grad_hidden, gate_values, up_values):
    sigmoid_gate = jax.nn.sigmoid(gate_values)
    grad_gate = (
        grad_hidden * up_values * sigmoid_gate * (1.0 + gate_values * (1.0 - sigmoid_gate))
    ).astype(jnp.bfloat16)
    grad_up = (grad_hidden * gate_values * sigmoid_gate).astype(jnp.bfloat16)
    return jnp.stack([grad_gate, grad_up])


def activate(gate_values, up_values):
    return (gate_values * jax.nn.sigmoid(gate_values) * up_values).astype(jnp.bfloat16)


def local(tokens, cotangent, gate_weight, up_weight, down_weight, gate_mask, up_mask, down_mask):
    gate_kept = apply_blocks(gate_weight, gate_mask)
    up_kept = apply_blocks(up_weight, up_mask)
    down_kept = apply_blocks(down_weight, down_mask)
    token_all, upstream_all = (
        lax.all_gather(tokens, "row", axis=0, tiled=True),
        lax.all_gather(cotangent, "row", axis=0, tiled=True),
    )
    paired = jnp.stack([gate_kept, up_kept])
    partial_value = jnp.einsum("td,kdf->ktf", token_all, paired, preferred_element_type=jnp.float32)
    back_partial = jnp.einsum(
        "td,fd->tf", upstream_all, down_kept, preferred_element_type=jnp.float32
    )
    totals = column_share(partial_value)
    hidden = activate(totals[0], totals[1])
    hidden_all = column_rows(hidden[None])[0]
    grad_hidden = column_share(back_partial[None])[0]
    grad_all = column_rows(gate_grads(grad_hidden, totals[0], totals[1]))
    out_part = jnp.dot(hidden_all, down_kept, preferred_element_type=jnp.float32)
    output = feature_share(out_part).astype(jnp.bfloat16)
    back_tokens = jnp.einsum("ktf,kdf->td", grad_all, paired, preferred_element_type=jnp.float32)
    grad_tokens = feature_share(back_tokens).astype(jnp.bfloat16)
    weight_grads = jnp.einsum(
        "td,ktf->kdf", token_all, grad_all, preferred_element_type=jnp.float32
    )
    grad_gate_weight = apply_blocks(weight_grads[0], gate_mask).astype(jnp.bfloat16)
    grad_up_weight = apply_blocks(weight_grads[1], up_mask).astype(jnp.bfloat16)
    down_grad = jnp.einsum(
        "tf,td->fd", hidden_all, upstream_all, preferred_element_type=jnp.float32
    )
    grad_down_weight = apply_blocks(down_grad, down_mask).astype(jnp.bfloat16)
    return (output, grad_tokens, grad_gate_weight, grad_up_weight, grad_down_weight)


def solution(mesh):
    return jax.shard_map(
        local,
        mesh=mesh,
        in_specs=(
            P("row", "col"),
            P("row", "col"),
            P("col", "row"),
            P("col", "row"),
            P("row", "col"),
            P("col", "row"),
            P("col", "row"),
            P("row", "col"),
        ),
        out_specs=(
            P("row", "col"),
            P("row", "col"),
            P("col", "row"),
            P("col", "row"),
            P("row", "col"),
        ),
        check_vma=False,
    )
```

profile of v0, /device:TPU:0, one launch (start us, length us, event | category | flops | bytes accessed | tf_op | source)
XLA Modules:
  0.0 427.6 jit_solution(1700836814638350203)
XLA Ops:
  8.7 0.8 fusion.12
  9.5 48.5 %all-gather.9.cloned.1.call-done = bf16[1024,1024]{1,0:T(8,128)(2,1)} async-done(((bf16[64,1024]{1,0:T(8,128)(2,1)}), bf16[1024,1024]{1,0:T(8,128)(2,1)}) %all-gather.9.cloned.1.call-update) | async-done | bytes 2097168 | tf_op jit(solution)/shard_map/all_gather | solution.py:46
  58.3 1.2 copy-done.2
  59.5 5.7 %convolution_bitcast_fusion.2 = f32[1,1024,896]{1,2,0:T(8,128)} fusion(bf16[1024,1024]{1,0:T(8,128)(2,1)} %all-gather.9.cloned.1.call-done, bf16[896,1024]{1,0:T(8,128)(2,1)S(1)} %copy-done.9, bf16[112,8,8,128]{3,2,1,0:T(8,128)(2,1)S(1)} %bitcast.98), kind=kOutput, calls=%fused_computation.14 | convolution fusion | flops 1879965696 | bytes 9437184 | tf_op jit(solution)/shard_map/td,fd->tf/dot_general | solution.py:50
  65.3 2.9 copy.27
  68.3 3.8 copy.25
  72.8 0.9 copy-done
  73.7 2.4 fusion.6
  76.1 28.6 %all-gather.5.cloned.1.call-done = bf16[1024,1024]{1,0:T(8,128)(2,1)} async-done(((bf16[64,1024]{1,0:T(8,128)(2,1)}), bf16[1024,1024]{1,0:T(8,128)(2,1)}) %all-gather.5.cloned.1.call-update) | async-done | bytes 2097168 | tf_op jit(solution)/shard_map/all_gather | solution.py:45
  104.7 9.7 %convolution_bitcast_fusion.1 = f32[2,1024,896]{1,2,0:T(8,128)} fusion(bf16[1,1024,896]{1,2,0:T(8,128)(2,1)} %get-tuple-element.26, bf16[1,1024,896]{1,2,0:T(8,128)(2,1)} %get-tuple-element.27, bf16[1024,1024]{1,0:T(8,128)(2,1)} %all-gather.5.cloned.1.call-done), kind=kOutput, calls=%fused_computation.9 | convolution fusion | flops 3759931392 | bytes 13107200 | tf_op jit(solution)/shard_map/td,kdf->ktf/dot_general | solution.py:49
  114.4 28.8 %reduce-scatter.9.cloned.1.call-done = f32[1,128,896]{1,2,0:T(8,128)} async-done(((f32[1,1024,896]{1,2,0:T(8,128)}), f32[1,128,896]{1,2,0:T(8,128)}) %reduce-scatter.9.cloned.1.call-update) | async-done | bytes 458768 | tf_op jit(solution)/shard_map/reduce_scatter | solution.py:16
  143.2 48.5 %reduce-scatter.5.cloned.1.call-done = f32[2,128,896]{1,2,0:T(8,128)} async-done(((f32[2,1024,896]{1,2,0:T(8,128)}), f32[2,128,896]{1,2,0:T(8,128)}) %reduce-scatter.5.cloned.1.call-update) | async-done | bytes 917520 | tf_op jit(solution)/shard_map/reduce_scatter | solution.py:16
  191.7 2.3 multiply_convert_fusion.2
  194.1 0.8 pad_maximum_fusion.5
  194.9 24.9 %all-gather.7.cloned.1.call-done = bf16[1,1024,896]{1,2,0:T(8,128)(2,1)} async-done(((bf16[1,128,896]{1,2,0:T(8,128)(2,1)}), bf16[1,1024,896]{1,2,0:T(8,128)(2,1)}) %all-gather.7.cloned.1.call-update) | async-done | bytes 1835024 | tf_op jit(solution)/shard_map/all_gather | solution.py:20
  219.9 6.5 %fusion.8 = f32[1024,1024]{1,0:T(8,128)} fusion(bf16[1,1024,896]{1,2,0:T(8,128)(2,1)} %all-gather.7.cloned.1.call-done, bf16[896,1024]{1,0:T(8,128)(2,1)} %param.12, bf16[112,8,8,128]{3,2,1,0:T(8,128)(2,1)S(1)} %bitcast.99), kind=kOutput, calls=%fused_computation.21 | convolution fusion | flops 1879965696 | bytes 9699328 | tf_op jit(solution)/shard_map/dot_general | solution.py:58
  226.6 29.6 %all-gather.11.cloned.1.call-done = bf16[2,1024,896]{1,2,0:T(8,128)(2,1)} async-done(((bf16[2,128,896]{1,2,0:T(8,128)(2,1)}), bf16[2,1024,896]{1,2,0:T(8,128)(2,1)}) %all-gather.11.cloned.1.call-update) | async-done | bytes 3670032 | tf_op jit(solution)/shard_map/all_gather | solution.py:20
  256.3 8.6 %fusion.3 = f32[1024,1024]{1,0:T(8,128)} fusion(bf16[2,1024,896]{1,2,0:T(8,128)(2,1)} %all-gather.11.cloned.1.call-done, bf16[1,1024,896]{1,2,0:T(8,128)(2,1)S(1)} %copy-done.4, bf16[1,1024,896]{1,2,0:T(8,128)(2,1)} %get-tuple-element.27), kind=kOutput, calls=%fused_computation.11 | convolution fusion | flops 3759931392 | bytes 11534336 | tf_op jit(solution)/shard_map/ktf,kdf->td/dot_general | solution.py:60
  265.1 1.4 copy-done.1
  266.5 2.6 copy.32
  269.1 4.4 %multiply_convert_fusion = bf16[7,128,8,128]{3,1,2,0:T(8,128)(2,1)S(1)} fusion(bf16[7,128,1024,1]{2,1,3,0:T(8,128)(2,1)} %bitcast.100, bf16[8,128,1024,1]{2,1,0,3:T(8,128)(2,1)} %bitcast.96, f32[7,8]{1,0:T(8,128)S(1)} %get-tuple-element.20), kind=kOutput, calls=%fused_computation.7 | convolution fusion | flops 1880883200 | bytes 5767392 | tf_op jit(solution)/shard_map/tf,td->fd/dot_general | solution.py:67
  273.5 1.2 copy.33
  274.7 1.8 copy.53
  276.5 1.1 copy-done.7
  277.5 6.0 %convolution_bitcast_fusion = f32[2,1024,896]{1,2,0:T(8,128)} fusion(bf16[2,1024,896]{1,2,0:T(8,128)(2,1)S(1)} %copy-done.7, bf16[1024,1024]{1,0:T(8,128)(2,1)S(1)} %copy-done.8), kind=kOutput, calls=%fused_computation.8 | convolution fusion | flops 3758096384 | bytes 13107200 | tf_op jit(solution)/shard_map/td,ktf->kdf/dot_general | solution.py:62
  284.1 5.8 %fusion = (bf16[1024,896]{0,1:T(8,128)(2,1)S(1)}, bf16[1024,896]{0,1:T(8,128)(2,1)}) fusion(f32[112,8,8,128]{3,2,1,0:T(8,128)S(1)} %bitcast.90, f32[2,1024,896]{1,2,0:T(8,128)} %convolution_bitcast_fusion, f32[112,8,8,128]{3,2,1,0:T(8,128)S(1)} %bitcast.91), kind=kLoop, calls=%fused_computation.1 | loop fusion | flops 3670016 | bytes 18350080 | tf_op jit(solution)/shard_map/convert_element_type | solution.py:66
  289.9 3.8 copy.34
  293.8 2.4 copy.35
  296.2 42.2 %reduce-scatter.7.cloned.1.call-done = f32[64,1024]{1,0:T(8,128)} async-done(((f32[1024,1024]{1,0:T(8,128)}), f32[64,1024]{1,0:T(8,128)}) %reduce-scatter.7.cloned.1.call-update) | async-done | bytes 262160 | tf_op jit(solution)/shard_map/reduce_scatter | solution.py:24
  338.4 1.6 convert_element_type.52
  340.1 79.0 %reduce-scatter.11.cloned.1.call-done = f32[64,1024]{1,0:T(8,128)} async-done(((f32[1024,1024]{1,0:T(8,128)}), f32[64,1024]{1,0:T(8,128)}) %reduce-scatter.11.cloned.1.call-update) | async-done | bytes 262160 | tf_op jit(solution)/shard_map/reduce_scatter | solution.py:24
  419.1 1.6 convert_element_type.55
  (43 shorter events, 3.9 us)
Async XLA Ops:
  7.2 52.3 %copy-start.9 = (bf16[896,1024]{1,0:T(8,128)(2,1)S(1)}, bf16[896,1024]{1,0:T(8,128)(2,1)}, u32[]{:S(2)}) copy-start(bf16[896,1024]{1,0:T(8,128)(2,1)} %param.12) | copy-start | bytes 5505028
  7.2 50.8 %all-gather.9.cloned.1.call-start = ((), (), s32[]{:S(2)}) async-start(), calls=%async_computation.8 | async-start | bytes 2228224 | tf_op jit(solution)/shard_map/all_gather | solution.py:46
  7.9 96.8 %all-gather.5.cloned.1.call-start = ((), (), s32[]{:S(2)}) async-start(), calls=%async_computation.4 | async-start | bytes 2228224 | tf_op jit(solution)/shard_map/all_gather | solution.py:45
  8.7 134.6 %reduce-scatter.9.cloned.1.call-start = ((), (), s32[]{:S(2)}) async-start(), calls=%async_computation.9 | async-start | bytes 4128768 | tf_op jit(solution)/shard_map/reduce_scatter | solution.py:16
  58.3 1.2 copy-start.2
  65.2 3.0 copy-start.5
  65.2 126.5 %reduce-scatter.5.cloned.1.call-start = ((), (), s32[]{:S(2)}) async-start(), calls=%async_computation.5 | async-start | bytes 8257536 | tf_op jit(solution)/shard_map/reduce_scatter | solution.py:16
  68.3 3.8 copy-start.6
  72.2 1.5 copy-start
  114.3 105.6 %copy-start.3 = (bf16[7,128,8,128]{3,2,1,0:T(8,128)(2,1)S(1)}, bf16[7,128,8,128]{3,2,1,0:T(8,128)(2,1)}, u32[]{:S(2)}) copy-start(bf16[7,128,8,128]{3,2,1,0:T(8,128)(2,1)} %copy-done.2) | copy-start | bytes 5505028
  114.3 105.5 %all-gather.7.cloned.1.call-start = ((), (), s32[]{:S(2)}) async-start(), calls=%async_computation.6 | async-start | bytes 2064384 | tf_op jit(solution)/shard_map/all_gather | solution.py:20
  194.0 62.3 %all-gather.11.cloned.1.call-start = ((), (), s32[]{:S(2)}) async-start(), calls=%async_computation.10 | async-start | bytes 4128768 | tf_op jit(solution)/shard_map/all_gather | solution.py:20
  194.9 143.5 %reduce-scatter.7.cloned.1.call-start = ((), (), s32[]{:S(2)}) async-start(), calls=%async_computation.7 | async-start | bytes 4456448 | tf_op jit(solution)/shard_map/reduce_scatter | solution.py:24
  226.4 29.9 %copy-start.4 = (bf16[1,1024,896]{1,2,0:T(8,128)(2,1)S(1)}, bf16[1,1024,896]{1,2,0:T(8,128)(2,1)}, u32[]{:S(2)}) copy-start(bf16[1,1024,896]{1,2,0:T(8,128)(2,1)} %get-tuple-element.26) | copy-start | bytes 5505028
  226.4 192.7 %reduce-scatter.11.cloned.1.call-start = ((), (), s32[]{:S(2)}) async-start(), calls=%async_computation.11 | async-start | bytes 4456448 | tf_op jit(solution)/shard_map/reduce_scatter | solution.py:24
  264.9 1.6 copy-start.1
  273.5 3.0 copy-start.8
  274.7 2.8 copy-start.7
Sparse Core Ops, SparseCore 0:
  10.2 47.7 all-gather.8
  60.1 44.5 all-gather.4
  107.1 36.0 reduce-scatter.8
  145.5 46.1 reduce-scatter.4
  194.1 25.7 all-gather.6
  221.4 34.8 all-gather.10
  259.6 78.7 reduce-scatter.6
  342.1 76.9 reduce-scatter.10
where the time goes:
time: 428 us
  waiting for transfers between devices  332 us (78%)
  matrix products  40.8 us (10%)
  local copies, waits for them, and re-layouts  24.9 us (6%)
  other arithmetic  15.3 us (4%)
  between operations  14.3 us (3%)
    reduce_scatter x2, waiting for transfers between devices, feature_share(): return lax.psum_scatter(values, 'row', scatter_dimension=0, tiled=True)  121 us
    reduce_scatter x2, waiting for transfers between devices, column_share(): return lax.psum_scatter(values, 'col', scatter_dimension=1, tiled=True)  77.3 us
    all_gather x2, waiting for transfers between devices, column_rows(): return lax.all_gather(values, 'col', axis=1, tiled=True)  54.6 us
    all_gather x1, waiting for transfers between devices, local(): lax.all_gather(cotangent, 'row', axis=0, tiled=True)  48.5 us
    all_gather x1, waiting for transfers between devices, local(): lax.all_gather(tokens, 'row', axis=0, tiled=True)  28.6 us
    unnamed x25, local copies, waits for them, and re-layouts  19.3 us
    dot_general x1, matrix products, local(): jnp.einsum('td,kdf->ktf', token_all, paired, preferred_element_type=jnp.f...  9.65 us
    dot_general x1, matrix products, local(): jnp.einsum('ktf,kdf->td', grad_all, paired, preferred_element_type=jnp.fl...  8.62 us
  transfers between devices with their start and end apart: 8, of which 8 were waited for; matrix products, arithmetic and copies ran while one was open for 17% of the time, Pallas kernels for 0%

commit v1 on v0

v1 whole, which is shorter than its diff:
```python
import functools

import jax
import jax.numpy as jnp
from jax import lax
from jax.experimental import pallas as pl
from jax.experimental.pallas import tpu as pltpu
from jax.sharding import PartitionSpec as P

BLOCK = 128
MESH = pl.DeviceIdType.MESH
F32 = jnp.float32
BF16 = jnp.bfloat16


def column_tiles(width):
    return [(at, min(256, width - at)) for at in range(0, width, 256)]


def kernel(
    dims,
    tok_ref, cot_ref, gate_hbm, up_hbm, down_hbm, gate_mask, up_mask, down_mask,
    out_ref, grad_ref, dgate_hbm, dup_hbm, ddown_hbm,
    wg, wu, wd, act, part, rpart, xs, xr, hall, outp, r1, r2f, r2s, r2r, dg, du, dd,
    w_sem, dw_sem, ag1_s, ag1_r, ag2_s, ag2_r, cx_s, cx_r, rs_s, rs_r, gx_s, gx_r, cf_s, cf_r,
    p1_s, p1_r, p2_s, p2_r,
):
    Z, Y, X, N, R = dims
    T = Z * Y * R
    half = T // 2
    Q = half // X
    DL, FL = wg.shape
    row = lax.axis_index("row")
    col = lax.axis_index("col")
    z, y = row // Y, row % Y
    x, k = col // 2, col % 2

    def at_z(d):
        return (((z + d) % Z) * Y + y, col)

    def at_y(d):
        return (z * Y + (y + d) % Y, col)

    def at_x(d):
        return (row, ((x + d) % X) * 2 + k)

    other = (row, x * 2 + 1 - k)

    def remote(src, dst, ssem, rsem, where):
        return pltpu.make_async_remote_copy(
            src_ref=src, dst_ref=dst, send_sem=ssem, recv_sem=rsem, device_id=where, device_id_type=MESH
        )

    def ag1(c):
        mine = pl.ds(c * R, R)
        return [
            remote(tok_ref.at[mine], act.at[0, c, z, y], ag1_s.at[c, 0, d - 1], ag1_r.at[c, 0, d - 1], at_y(d))
            for d in range(1, Y)
        ] + [
            remote(cot_ref.at[mine], act.at[1, c, z, y], ag1_s.at[c, 1, d - 1], ag1_r.at[c, 1, d - 1], at_z(d))
            for d in range(1, Z)
        ]

    def ag2(c):
        tok = [
            remote(act.at[0, c, z], act.at[0, c, z], ag2_s.at[c, 0, d - 1], ag2_r.at[c, 0, d - 1], at_z(d))
            for d in range(1, Z)
        ]
        cot = [
            remote(act.at[1, c, :, y], act.at[1, c, :, y], ag2_s.at[c, 1, d - 1], ag2_r.at[c, 1, d - 1], at_y(d))
            for d in range(1, Y)
        ]
        return tok, cot

    def cx(c, j):
        return remote(
            part.at[c, j, pl.ds((1 - k) * half, half)], rpart.at[c, j], cx_s.at[c, j], cx_r.at[c, j], other
        )

    def rs(c):
        return [
            remote(xs.at[c, (x + d) % X], xr.at[c, d - 1], rs_s.at[c, d - 1], rs_r.at[c, d - 1], at_x(d))
            for d in range(1, X)
        ]

    def gx(c):
        mine = hall.at[c, k * X + x]
        return [remote(mine, mine, gx_s.at[c, d - 1], gx_r.at[c, d - 1], at_x(d)) for d in range(1, X)]

    def cf(c, d):
        block = hall.at[c, k * X + (x + X - d) % X]
        return remote(block, block, cf_s.at[c, d], cf_r.at[c, d], other)

    def p1(c):
        out = [
            remote(outp.at[c, 0, (z + d) % Z], r1.at[c, 0, d - 1], p1_s.at[c, 0, d - 1], p1_r.at[c, 0, d - 1], at_z(d))
            for d in range(1, Z)
        ]
        grad = [
            remote(outp.at[c, 1, :, (y + d) % Y], r1.at[c, 1, d - 1], p1_s.at[c, 1, d - 1], p1_r.at[c, 1, d - 1], at_y(d))
            for d in range(1, Y)
        ]
        return out, grad

    def p2(c):
        out = [
            remote(r2s.at[c, 0, (y + d) % Y], r2r.at[c, 0, d - 1], p2_s.at[c, 0, d - 1], p2_r.at[c, 0, d - 1], at_y(d))
            for d in range(1, Y)
        ]
        grad = [
            remote(r2s.at[c, 1, (z + d) % Z], r2r.at[c, 1, d - 1], p2_s.at[c, 1, d - 1], p2_r.at[c, 1, d - 1], at_z(d))
            for d in range(1, Z)
        ]
        return out, grad

    def start(copies):
        for copy in copies:
            copy.start()

    def recv(copies):
        for copy in copies:
            copy.wait_recv()

    loads = [
        pltpu.make_async_copy(src, dst, w_sem.at[i])
        for i, (src, dst) in enumerate(((gate_hbm, wg), (up_hbm, wu), (down_hbm, wd)))
    ]
    start(loads)
    peers = [other] + [at_x(d) for d in range(1, X)] + [at_y(d) for d in range(1, Y)] + [at_z(d) for d in range(1, Z)]
    barrier = pltpu.get_barrier_semaphore()
    for peer in peers:
        pl.semaphore_signal(barrier, inc=1, device_id=peer, device_id_type=MESH)
    pl.semaphore_wait(barrier, len(peers))

    start(ag1(0))
    for c in range(N):
        act[0, c, z, y] = tok_ref[c * R : (c + 1) * R, :]
        act[1, c, z, y] = cot_ref[c * R : (c + 1) * R, :]
    if N > 1:
        start(ag1(1))

    def gather_on(c):
        recv(ag1(c))
        tok, cot = ag2(c)
        start(tok)
        start(cot)

    gather_on(0)

    for copy, weight, mask in zip(loads, (wg, wu, wd), (gate_mask, up_mask, down_mask)):
        copy.wait()
        high, wide = weight.shape[0] // BLOCK, weight.shape[1] // BLOCK

        def keep_row(i, _, weight=weight, mask=mask, wide=wide):
            rows = pl.ds(pl.multiple_of(i * BLOCK, BLOCK), BLOCK)
            for j in range(wide):
                cols = slice(j * BLOCK, (j + 1) * BLOCK)
                kept = jnp.full((BLOCK, BLOCK), mask[i, j], jnp.int32).astype(F32).astype(BF16)
                weight[rows, cols] = weight[rows, cols] * kept
            return 0

        lax.fori_loop(0, high, keep_row, 0)

    def forward(c):
        tok, cot = ag2(c)
        recv(tok)
        for j, weight in enumerate((wg, wu)):
            tokens = act[0, c].reshape(T, DL)
            for at, width in column_tiles(FL):
                part[c, j, :, at : at + width] = jnp.dot(
                    tokens, weight[:, at : at + width], preferred_element_type=F32
                )
            cx(c, j).start()
        recv(cot)
        upstream = act[1, c].reshape(T, DL)
        for at, width in column_tiles(FL):
            part[c, 2, :, at : at + width] = lax.dot_general(
                upstream, wd[at : at + width, :], (((1,), (1,)), ((), ())), preferred_element_type=F32
            )
        cx(c, 2).start()

    def share(c):
        for j in range(3):
            cx(c, j).wait_recv()
            for b in range(X):
                total = part[c, j, pl.ds(k * half + b * Q, Q), :] + rpart[c, j, b * Q : (b + 1) * Q, :]
                xs[c, b, j] = total.astype(BF16)
        start(rs(c))

    def activate(c):
        recv(rs(c))

        def total(j):
            value = part[c, j, pl.ds(k * half + x * Q, Q), :] + rpart[c, j, pl.ds(x * Q, Q), :]
            for d in range(1, X):
                value = value + xr[c, d - 1, j].astype(F32)
            return value

        gate, up, back = total(0), total(1), total(2)
        s = 1.0 / (1.0 + jnp.exp(-gate))
        block = k * X + x
        hall[c, block, 0] = (gate * s * up).astype(BF16)
        hall[c, block, 1] = (back * up * s * (1.0 + gate * (1.0 - s))).astype(BF16)
        hall[c, block, 2] = (back * gate * s).astype(BF16)
        start(gx(c))
        cf(c, 0).start()

    def pass_on(c):
        for d, copy in enumerate(gx(c)):
            copy.wait_recv()
            cf(c, d + 1).start()

    def backward(c):
        for d in range(X):
            cf(c, d).wait_recv()
        out, grad = p1(c)
        hidden = hall[c, :, 0].reshape(T, FL)
        for at, width in column_tiles(DL):
            value = jnp.dot(hidden, wd[:, at : at + width], preferred_element_type=F32)
            outp[c, 0, :, :, :, at : at + width] = value.astype(BF16).reshape(Z, Y, R, width)
        start(out)
        grad_gate = hall[c, :, 1].reshape(T, FL)
        grad_up = hall[c, :, 2].reshape(T, FL)
        for at, width in column_tiles(DL):
            nt = (((1,), (1,)), ((), ()))
            value = lax.dot_general(grad_gate, wg[at : at + width, :], nt, preferred_element_type=F32)
            value += lax.dot_general(grad_up, wu[at : at + width, :], nt, preferred_element_type=F32)
            outp[c, 1, :, :, :, at : at + width] = value.astype(BF16).reshape(Z, Y, R, width)
        start(grad)

    def narrow(c):
        out, grad = p1(c)
        send_out, send_grad = p2(c)
        recv(out)
        for b in range(Y):
            value = outp[c, 0, z, b].astype(F32)
            for d in range(1, Z):
                value = value + r1[c, 0, d - 1, b].astype(F32)
            r2f[c, 0, b] = value
            r2s[c, 0, b] = value.astype(BF16)
        start(send_out)
        recv(grad)
        for b in range(Z):
            value = outp[c, 1, b, y].astype(F32)
            for d in range(1, Y):
                value = value + r1[c, 1, d - 1, b].astype(F32)
            r2f[c, 1, b] = value
            r2s[c, 1, b] = value.astype(BF16)
        start(send_grad)

    def finish(c):
        out, grad = p2(c)
        rows = pl.ds(pl.multiple_of(c * R, R), R)
        recv(out)
        value = r2f[c, 0, y]
        for d in range(1, Y):
            value = value + r2r[c, 0, d - 1].astype(F32)
        out_ref[rows, :] = value.astype(BF16)
        recv(grad)
        value = r2f[c, 1, z]
        for d in range(1, Z):
            value = value + r2r[c, 1, d - 1].astype(F32)
        grad_ref[rows, :] = value.astype(BF16)

    def tick(t, _):
        def when(c, stage):
            @pl.when((c >= 0) & (c < N))
            def _():
                stage(c)

        when(t + 2, lambda c: start(ag1(c)))
        when(t + 1, gather_on)
        when(t, forward)
        when(t, share)
        when(t - 1, activate)
        when(t - 2, pass_on)
        when(t - 2, backward)
        when(t - 3, narrow)
        when(t - 4, finish)
        return 0

    lax.fori_loop(0, N + 2, tick, 0)

    writes = []

    def weight_grad(staged, lhs, rhs, mask, hbm, n):
        high, wide = staged.shape

        def strip(i, _):
            rows = pl.ds(pl.multiple_of(i * BLOCK, BLOCK), BLOCK)
            left = lhs(rows)
            for at, width in column_tiles(wide):
                value = lax.dot_general(left, rhs(at, width), (((0,), (0,)), ((), ())), preferred_element_type=F32)
                for b in range(0, width, BLOCK):
                    kept = jnp.full((BLOCK, BLOCK), mask[i, (at + b) // BLOCK], jnp.int32).astype(F32)
                    staged[rows, at + b : at + b + BLOCK] = (value[:, b : b + BLOCK] * kept).astype(BF16)
            return 0

        lax.fori_loop(0, high // BLOCK, strip, 0)
        copy = pltpu.make_async_copy(staged, hbm, dw_sem.at[n])
        copy.start()
        writes.append(copy)

    everything = N * T

    def grads_of(j):
        return lambda at, width: hall[:, :, j, :, at : at + width].reshape(everything, width)

    def tokens_of(rows):
        return act[0, :, :, :, :, rows].reshape(everything, BLOCK)

    weight_grad(dg, tokens_of, grads_of(1), gate_mask, dgate_hbm, 0)
    weight_grad(du, tokens_of, grads_of(2), up_mask, dup_hbm, 1)
    narrow(N - 1)
    if N > 1:
        finish(N - 2)
    weight_grad(
        dd,
        lambda rows: hall[:, :, 0, :, rows].reshape(everything, BLOCK),
        lambda at, width: act[1, :, :, :, :, at : at + width].reshape(everything, width),
        down_mask,
        ddown_hbm,
        2,
    )
    finish(N - 1)

    def drain(c, _):
        for copies in (ag1(c), *ag2(c), [cx(c, j) for j in range(3)], rs(c), gx(c), [cf(c, d) for d in range(X)], *p1(c), *p2(c)):
            for copy in copies:
                copy.wait_send()
        return 0

    lax.fori_loop(0, N, drain, 0)
    for copy in writes:
        copy.wait()


def local(dims, tokens, cotangent, gate_weight, up_weight, down_weight, gate_mask, up_mask, down_mask):
    Z, Y, X, N, R = dims
    T = Z * Y * R
    DL, FL = gate_weight.shape
    half, Q = T // 2, T // 2 // X
    vmem, smem, hbm = (pl.BlockSpec(memory_space=s) for s in (pltpu.VMEM, pltpu.SMEM, pl.ANY))
    dma = pltpu.SemaphoreType.DMA
    zy = max(Z, Y)
    ax = max(zy - 1, 1)
    xx = max(X - 1, 1)
    return pl.pallas_call(
        functools.partial(kernel, dims),
        out_shape=(
            jax.ShapeDtypeStruct(tokens.shape, BF16),
            jax.ShapeDtypeStruct(tokens.shape, BF16),
            jax.ShapeDtypeStruct((DL, FL), BF16),
            jax.ShapeDtypeStruct((DL, FL), BF16),
            jax.ShapeDtypeStruct((FL, DL), BF16),
        ),
        in_specs=[vmem, vmem, hbm, hbm, hbm, smem, smem, smem],
        out_specs=(vmem, vmem, hbm, hbm, hbm),
        scratch_shapes=[
            pltpu.VMEM((DL, FL), BF16),
            pltpu.VMEM((DL, FL), BF16),
            pltpu.VMEM((FL, DL), BF16),
            pltpu.VMEM((2, N, Z, Y, R, DL), BF16),
            pltpu.VMEM((N, 3, T, FL), F32),
            pltpu.VMEM((N, 3, half, FL), F32),
            pltpu.VMEM((N, X, 3, Q, FL), BF16),
            pltpu.VMEM((N, xx, 3, Q, FL), BF16),
            pltpu.VMEM((N, 2 * X, 3, Q, FL), BF16),
            pltpu.VMEM((N, 2, Z, Y, R, DL), BF16),
            pltpu.VMEM((N, 2, ax, zy, R, DL), BF16),
            pltpu.VMEM((N, 2, zy, R, DL), F32),
            pltpu.VMEM((N, 2, zy, R, DL), BF16),
            pltpu.VMEM((N, 2, ax, R, DL), BF16),
            pltpu.VMEM((DL, FL), BF16),
            pltpu.VMEM((DL, FL), BF16),
            pltpu.VMEM((FL, DL), BF16),
            dma((3,)),
            dma((3,)),
            *[dma((N, 2, ax))] * 4,
            *[dma((N, 3))] * 2,
            *[dma((N, xx))] * 2,
            *[dma((N, xx))] * 2,
            *[dma((N, X))] * 2,
            *[dma((N, 2, ax))] * 4,
        ],
        compiler_params=pltpu.CompilerParams(
            collective_id=0, has_side_effects=True, vmem_limit_bytes=60 * 2**20
        ),
    )(tokens, cotangent, gate_weight, up_weight, down_weight, gate_mask, up_mask, down_mask)


def solution(mesh, dims=(4, 4, 4, 4, 16)):
    return jax.shard_map(
        functools.partial(local, dims),
        mesh=mesh,
        in_specs=(
            P("row", "col"),
            P("row", "col"),
            P("col", "row"),
            P("col", "row"),
            P("row", "col"),
            P("col", "row"),
            P("col", "row"),
            P("row", "col"),
        ),
        out_specs=(
            P("row", "col"),
            P("row", "col"),
            P("col", "row"),
            P("col", "row"),
            P("row", "col"),
        ),
        check_vma=False,
    )
```

time: 428 us -> 118 us (0.28)
  waiting for transfers between devices: 332 us -> 0 us
  Pallas kernels: 0 us -> 107 us
  matrix products: 40.8 us -> 0 us
  local copies, waits for them, and re-layouts: 24.9 us -> 9.53 us
  other arithmetic: 15.3 us -> 0 us
  between operations: 14.3 us -> 0.65 us
    reduce_scatter x4 -> x0, waiting for transfers between devices: 199 us -> none  [the longest x2 121 us: feature_share(): return lax.psum_scatter(values, 'row', scatter_dimension=0, tiled=True)]
    all_gather x4 -> x0, waiting for transfers between devices: 132 us -> none  [the longest x2 54.6 us: column_rows(): return lax.all_gather(values, 'col', axis=1, tiled=True)]
    pallas_call x0 -> x1, Pallas kernels: none -> 107 us  [local(): pl.pallas_call(functools.partial(kernel, dims), out_shape=(jax.ShapeDtype...]
    dot_general x6 -> x0, matrix products: 40.8 us -> none  [the longest x1 9.65 us: local(): jnp.einsum('td,kdf->ktf', token_all, paired, preferred_element_type=jnp.f...]
    convert_element_type x7 -> x0, other arithmetic: 12.1 us -> none  [the longest x1 5.81 us: local(): grad_up_weight = apply_blocks(weight_grads[1], up_mask).astype(jnp.bfloat16)]
    unnamed x25 -> x9, local copies, waits for them, and re-layouts: 19.3 us -> 9.53 us
  transfers between devices with their start and end apart: 8 -> 0, of which waited for: 8 -> 0; matrix products, arithmetic and copies ran while one was open for 17% -> 0% of each run, Pallas kernels for 0% -> 0%
where the time goes in v1:
time: 118 us; the launch traced here: 117 us
  Pallas kernels  107 us (91%)
  local copies, waits for them, and re-layouts  9.53 us (8%)
    pallas_call x1, Pallas kernels, local(): pl.pallas_call(functools.partial(kernel, dims), out_shape=(jax.ShapeDtype...  107 us
    unnamed x9, local copies, waits for them, and re-layouts  9.53 us

profile of v1, /device:TPU:0, one launch (start us, length us, event | category | flops | bytes accessed | tf_op | source)
XLA Modules:
  0.0 117.5 jit_solution(7264321795659513004)
XLA Ops:
  0.6 107.3 %shard_map.119 = (bf16[64,1024]{1,0:T(8,128)(2,1)}, bf16[64,1024]{1,0:T(8,128)(2,1)}, bf16[1024,896]{1,0:T(8,128)(2,1)}, bf16[1024,896]{1,0:T(8,128)(2,1)}, bf16[896,1024]{1,0:T(8,128)(2,1)}) custom-call(bf16[64,1024]{1,0:T(8,128)(2,1)} %tok_ref.1, bf16[64,1024]{1,0:T(8,128)(2,1)} %cot_ref.1, bf16[1024,896]{1,0:T(8,128)(2,1)} %gate_hbm.1, ...), custom_call_target="tpu_custom_call" | custom-call | tf_op jit(solution)/shard_map/pallas_call | solution.py:348
  108.0 1.6 %copy.18 = bf16[64,1024]{1,0:T(8,128)(2,1)} copy(bf16[64,1024]{1,0:T(8,128)(2,1)} %get-tuple-element.10) | data formatting | bytes 262144
  109.5 1.6 %copy.19 = bf16[64,1024]{1,0:T(8,128)(2,1)} copy(bf16[64,1024]{1,0:T(8,128)(2,1)} %get-tuple-element.11) | data formatting | bytes 262144
  111.1 0.0 copy-start.1
  111.1 3.0 %copy.20 = bf16[1024,896]{1,0:T(8,128)(2,1)} copy(bf16[1024,896]{1,0:T(8,128)(2,1)} %get-tuple-element.12) | data formatting | bytes 3670016
  114.1 0.0 copy-done.1
  114.1 0.0 copy-start
  114.1 1.2 %copy.21 = bf16[1024,896]{1,0:T(8,128)(2,1)} copy(bf16[1024,896]{1,0:T(8,128)(2,1)S(1)} %copy-done.1) | data formatting | bytes 3670016
  115.3 0.9 copy-done
  116.3 1.2 %copy.22 = bf16[896,1024]{1,0:T(8,128)(2,1)} copy(bf16[896,1024]{1,0:T(8,128)(2,1)S(1)} %copy-done) | data formatting | bytes 3670016
Async XLA Ops:
  111.1 3.0 %copy-start.1 = (bf16[1024,896]{1,0:T(8,128)(2,1)S(1)}, bf16[1024,896]{1,0:T(8,128)(2,1)}, u32[]{:S(2)}) copy-start(bf16[1024,896]{1,0:T(8,128)(2,1)} %get-tuple-element.13) | copy-start | bytes 5505028
  114.1 2.2 %copy-start = (bf16[896,1024]{1,0:T(8,128)(2,1)S(1)}, bf16[896,1024]{1,0:T(8,128)(2,1)}, u32[]{:S(2)}) copy-start(bf16[896,1024]{1,0:T(8,128)(2,1)} %get-tuple-element.14) | copy-start | bytes 5505028

commit v2 on v1

v2 whole, which is shorter than its diff:
```python
import functools

import jax
import jax.numpy as jnp
from jax import lax
from jax.experimental import pallas as pl
from jax.experimental.pallas import tpu as pltpu
from jax.sharding import PartitionSpec as P

BLOCK = 128
MESH = pl.DeviceIdType.MESH
F32 = jnp.float32
BF16 = jnp.bfloat16

ORDER = (
    ("gate_grads", ((0, 13),)),
    ("gather", ((2, 0), (3, 3))),
    ("forward", ((0, 1), (1, 2), (2, 3), (3, 5))),
    ("activate", ((0, 3), (1, 4), (2, 8), (3, 9))),
    ("gather_on", ((1, 0), (2, 1), (3, 3))),
    ("pass_on", ((0, 5), (1, 8), (2, 10), (3, 11))),
    ("relay", ((0, 2), (1, 3), (2, 6), (3, 7))),
    ("share", ((0, 1), (1, 2), (2, 3), (3, 5))),
    ("spread", ((0, 3), (1, 6), (2, 9), (3, 10))),
    ("narrow", ((0, 9), (1, 12), (2, 13), (3, 14))),
    ("up_grads", ((0, 12),)),
    ("down_grads", ((0, 14),)),
    ("backward", ((0, 6), (1, 9), (2, 10), (3, 11))),
    ("finish", ((0, 10), (1, 14), (2, 15), (3, 16))),
)
TICKS = 17


def column_tiles(width):
    return [(at, min(256, width - at)) for at in range(0, width, 256)]


def kernel(
    dims,
    tok_hbm, cot_hbm, gate_hbm, up_hbm, down_hbm, gate_mask, up_mask, down_mask,
    out_hbm, grad_hbm, dgate_hbm, dup_hbm, ddown_hbm,
    wg, wu, wd, act, part, rpart, xs, xq, xt, xr, hall, outp, r1, r2f, r2s, r2r, fin, dg, du, dd,
    own_sem, o_sem, w_sem, dw_sem, ag1_s, ag1_r, ag2_s, ag2_r, cx_s, cx_r, rs1_s, rs1_r, rs2_s, rs2_r, gx1_s, gx1_r, gx2_s, gx2_r, cf_s, cf_r,
    p1_s, p1_r, p2_s, p2_r,
):
    Z, Y, X, N, R = dims
    T = Z * Y * R
    half = T // 2
    Q = half // X
    H = Q // 2
    DL, FL = wg.shape
    row = lax.axis_index("row")
    col = lax.axis_index("col")
    z, y = row // Y, row % Y
    x, k = col // 2, col % 2

    def at_z(d):
        return (((z + d) % Z) * Y + y, col)

    def at_y(d):
        return (z * Y + (y + d) % Y, col)

    def at_x(d):
        return (row, ((x + d) % X) * 2 + k)

    other = (row, x * 2 + 1 - k)

    def remote(src, dst, ssem, rsem, where):
        return pltpu.make_async_remote_copy(
            src_ref=src, dst_ref=dst, send_sem=ssem, recv_sem=rsem, device_id=where, device_id_type=MESH
        )

    def ag1(c):
        return [
            remote(tok_hbm.at[c], act.at[0, c, z, y], ag1_s.at[c, 0, d - 1], ag1_r.at[c, 0, d - 1], at_y(d))
            for d in range(1, Y)
        ] + [
            remote(cot_hbm.at[c], act.at[1, c, z, y], ag1_s.at[c, 1, d - 1], ag1_r.at[c, 1, d - 1], at_z(d))
            for d in range(1, Z)
        ]

    def ag2(c):
        tok = [
            remote(act.at[0, c, z], act.at[0, c, z], ag2_s.at[c, 0, d - 1], ag2_r.at[c, 0, d - 1], at_z(d))
            for d in range(1, Z)
        ]
        cot = [
            remote(act.at[1, c, :, y], act.at[1, c, :, y], ag2_s.at[c, 1, d - 1], ag2_r.at[c, 1, d - 1], at_y(d))
            for d in range(1, Y)
        ]
        return tok, cot

    def cx(c, j):
        return remote(
            part.at[c, j, pl.ds((1 - k) * half, half)], rpart.at[c, j], cx_s.at[c, j], cx_r.at[c, j], other
        )

    def rs1(c):
        right, left, far = (x + 1) % X, (x + X - 1) % X, (x + 2) % X
        moves = (
            (xs.at[c, far, 0], xq.at[c, 0], 1),
            (xs.at[c, far, 1], xq.at[c, 1], X - 1),
            (xs.at[c, right, 1], xr.at[c, 0], 1),
            (xs.at[c, left, 0], xr.at[c, 1], X - 1),
        )
        return [remote(src, dst, rs1_s.at[c, i], rs1_r.at[c, i], at_x(d)) for i, (src, dst, d) in enumerate(moves)]

    def rs2(c):
        return [
            remote(xt.at[c, i], xr.at[c, 2 + i], rs2_s.at[c, i], rs2_r.at[c, i], at_x(d)) for i, d in ((0, 1), (1, X - 1))
        ]

    def gx1(c):
        mine = hall.at[c, k * X + x]
        return [remote(mine, mine, gx1_s.at[c, i], gx1_r.at[c, i], at_x(d)) for i, d in ((0, 1), (1, X - 1))]

    def gx2(c):
        copies = []
        for i, d in ((0, 1), (1, X - 1)):
            piece = hall.at[c, k * X + (x + X - d) % X, i]
            copies.append(remote(piece, piece, gx2_s.at[c, i], gx2_r.at[c, i], at_x(d)))
        return copies

    def cf(c, i):
        block = hall.at[c, k * X + (x + (0, X - 1, 1, 2)[i]) % X]
        return remote(block, block, cf_s.at[c, i], cf_r.at[c, i], other)

    def p1(c):
        out = [
            remote(outp.at[c, 0, (z + d) % Z], r1.at[c, 0, d - 1], p1_s.at[c, 0, d - 1], p1_r.at[c, 0, d - 1], at_z(d))
            for d in range(1, Z)
        ]
        grad = [
            remote(outp.at[c, 1, :, (y + d) % Y], r1.at[c, 1, d - 1], p1_s.at[c, 1, d - 1], p1_r.at[c, 1, d - 1], at_y(d))
            for d in range(1, Y)
        ]
        return out, grad

    def p2(c):
        out = [
            remote(r2s.at[c, 0, (y + d) % Y], r2r.at[c, 0, d - 1], p2_s.at[c, 0, d - 1], p2_r.at[c, 0, d - 1], at_y(d))
            for d in range(1, Y)
        ]
        grad = [
            remote(r2s.at[c, 1, (z + d) % Z], r2r.at[c, 1, d - 1], p2_s.at[c, 1, d - 1], p2_r.at[c, 1, d - 1], at_z(d))
            for d in range(1, Z)
        ]
        return out, grad

    def start(copies):
        for copy in copies:
            copy.start()

    def recv(copies):
        for copy in copies:
            copy.wait_recv()

    loads = [
        pltpu.make_async_copy(src, dst, w_sem.at[i])
        for i, (src, dst) in enumerate(((gate_hbm, wg), (up_hbm, wu), (down_hbm, wd)))
    ]
    own = [
        pltpu.make_async_copy(src, act.at[i, :, z, y], own_sem.at[i]) for i, src in enumerate((tok_hbm, cot_hbm))
    ]
    start(own)
    start(loads)
    peers = [other] + [at_x(d) for d in (1, X - 1)] + [at_y(d) for d in range(1, Y)] + [at_z(d) for d in range(1, Z)]
    barrier = pltpu.get_barrier_semaphore()
    for peer in peers:
        pl.semaphore_signal(barrier, inc=1, device_id=peer, device_id_type=MESH)
    pl.semaphore_wait(barrier, len(peers))

    def gather(c):
        start(ag1(c))

    def gather_on(c):
        recv(ag1(c))
        tok, cot = ag2(c)
        start(tok)
        start(cot)

    gather(0)
    gather(1)
    for copy in own:
        copy.wait()
    gather_on(0)

    for copy, weight, mask in zip(loads, (wg, wu, wd), (gate_mask, up_mask, down_mask)):
        copy.wait()
        high, wide = weight.shape[0] // BLOCK, weight.shape[1] // BLOCK

        def keep_row(i, _, weight=weight, mask=mask, wide=wide):
            rows = pl.ds(pl.multiple_of(i * BLOCK, BLOCK), BLOCK)
            for j in range(wide):
                cols = slice(j * BLOCK, (j + 1) * BLOCK)
                kept = jnp.full((BLOCK, BLOCK), mask[i, j], jnp.int32).astype(F32).astype(BF16)
                weight[rows, cols] = weight[rows, cols] * kept
            return 0

        lax.fori_loop(0, high, keep_row, 0)

    def forward(c):
        tok, cot = ag2(c)
        recv(tok)
        for j, weight in enumerate((wg, wu)):
            tokens = act[0, c].reshape(T, DL)
            for at, width in column_tiles(FL):
                part[c, j, :, at : at + width] = jnp.dot(
                    tokens, weight[:, at : at + width], preferred_element_type=F32
                )
            cx(c, j).start()
        recv(cot)
        upstream = act[1, c].reshape(T, DL)
        for at, width in column_tiles(FL):
            part[c, 2, :, at : at + width] = lax.dot_general(
                upstream, wd[at : at + width, :], (((1,), (1,)), ((), ())), preferred_element_type=F32
            )
        cx(c, 2).start()

    def mine(c, j, b, h):
        at = pl.multiple_of(b * Q + h * H, H)
        here = pl.ds(pl.multiple_of(k * half + at, H), H)
        return part[c, j, here, :] + rpart[c, j, pl.ds(at, H), :]

    def share(c):
        for j in range(3):
            cx(c, j).wait_recv()
            for b in range(X):
                for h in range(2):
                    xs[c, b, h, j] = mine(c, j, b, h).astype(BF16)
        start(rs1(c))

    def relay(c):
        arriving, onward = rs1(c), rs2(c)
        for i, d in ((0, 1), (1, X - 1)):
            arriving[i].wait_recv()
            for j in range(3):
                xt[c, i, j] = (mine(c, j, (x + d) % X, i) + xq[c, i, j].astype(F32)).astype(BF16)
            onward[i].start()

    def activate(c):
        recv(rs1(c)[2:])
        recv(rs2(c))
        block = k * X + x
        for h in range(2):

            def total(j, h=h):
                return mine(c, j, x, h) + xr[c, 1 - h, j].astype(F32) + xr[c, 2 + h, j].astype(F32)

            gate, up, back = total(0), total(1), total(2)
            s = 1.0 / (1.0 + jnp.exp(-gate))
            hall[c, block, h, 0] = (gate * s * up).astype(BF16)
            hall[c, block, h, 1] = (back * up * s * (1.0 + gate * (1.0 - s))).astype(BF16)
            hall[c, block, h, 2] = (back * gate * s).astype(BF16)
        start(gx1(c))
        cf(c, 0).start()

    def spread(c):
        for i, (arriving, onward) in enumerate(zip(gx1(c), gx2(c))):
            arriving.wait_recv()
            onward.start()
            cf(c, 1 + i).start()

    def pass_on(c):
        recv(gx2(c))
        cf(c, 3).start()

    def backward(c):
        for i in range(4):
            cf(c, i).wait_recv()
        out, grad = p1(c)
        hidden = hall[c, :, :, 0].reshape(T, FL)
        for at, width in column_tiles(DL):
            value = jnp.dot(hidden, wd[:, at : at + width], preferred_element_type=F32)
            outp[c, 0, :, :, :, at : at + width] = value.astype(BF16).reshape(Z, Y, R, width)
        start(out)
        grad_gate = hall[c, :, :, 1].reshape(T, FL)
        grad_up = hall[c, :, :, 2].reshape(T, FL)
        for at, width in column_tiles(DL):
            nt = (((1,), (1,)), ((), ()))
            value = lax.dot_general(grad_gate, wg[at : at + width, :], nt, preferred_element_type=F32)
            value += lax.dot_general(grad_up, wu[at : at + width, :], nt, preferred_element_type=F32)
            outp[c, 1, :, :, :, at : at + width] = value.astype(BF16).reshape(Z, Y, R, width)
        start(grad)

    def narrow(c):
        out, grad = p1(c)
        send_out, send_grad = p2(c)
        recv(out)
        for b in range(Y):
            value = outp[c, 0, z, b].astype(F32)
            for d in range(1, Z):
                value = value + r1[c, 0, d - 1, b].astype(F32)
            r2f[c, 0, b] = value
            r2s[c, 0, b] = value.astype(BF16)
        start(send_out)
        recv(grad)
        for b in range(Z):
            value = outp[c, 1, b, y].astype(F32)
            for d in range(1, Y):
                value = value + r1[c, 1, d - 1, b].astype(F32)
            r2f[c, 1, b] = value
            r2s[c, 1, b] = value.astype(BF16)
        start(send_grad)

    def final(c):
        return [
            pltpu.make_async_copy(fin.at[i, c], dst.at[c], o_sem.at[i, c]) for i, dst in enumerate((out_hbm, grad_hbm))
        ]

    def finish(c):
        out, grad = p2(c)
        recv(out)
        value = r2f[c, 0, y]
        for d in range(1, Y):
            value = value + r2r[c, 0, d - 1].astype(F32)
        fin[0, c] = value.astype(BF16)
        recv(grad)
        value = r2f[c, 1, z]
        for d in range(1, Z):
            value = value + r2r[c, 1, d - 1].astype(F32)
        fin[1, c] = value.astype(BF16)
        start(final(c))

    def weight_grad(staged, lhs, rhs, mask, hbm, n):
        high, wide = staged.shape
        for top, tall in column_tiles(high):
            left = lhs(top, tall)
            for at, width in column_tiles(wide):
                value = lax.dot_general(left, rhs(at, width), (((0,), (0,)), ((), ())), preferred_element_type=F32)
                for a in range(0, tall, BLOCK):
                    for b in range(0, width, BLOCK):
                        kept = jnp.full((BLOCK, BLOCK), mask[(top + a) // BLOCK, (at + b) // BLOCK], jnp.int32).astype(F32)
                        staged[top + a : top + a + BLOCK, at + b : at + b + BLOCK] = (
                            value[a : a + BLOCK, b : b + BLOCK] * kept
                        ).astype(BF16)
        pltpu.make_async_copy(staged, hbm, dw_sem.at[n]).start()

    everything = N * T

    def grads_of(j):
        return lambda at, width: hall[:, :, :, j, :, at : at + width].reshape(everything, width)

    def tokens_of(at, width):
        return act[0, :, :, :, :, at : at + width].reshape(everything, width)

    def upstream_of(at, width):
        return act[1, :, :, :, :, at : at + width].reshape(everything, width)

    def gate_grads(_):
        weight_grad(dg, tokens_of, grads_of(1), gate_mask, dgate_hbm, 0)

    def up_grads(_):
        weight_grad(du, tokens_of, grads_of(2), up_mask, dup_hbm, 1)

    def down_grads(_):
        weight_grad(dd, grads_of(0), upstream_of, down_mask, ddown_hbm, 2)

    stages = {
        "gather": gather, "gather_on": gather_on, "forward": forward, "share": share, "relay": relay,
        "activate": activate, "spread": spread, "pass_on": pass_on, "backward": backward, "narrow": narrow,
        "finish": finish, "gate_grads": gate_grads, "up_grads": up_grads, "down_grads": down_grads,
    }

    def tick(t, _):
        for name, ticks in ORDER:
            c, now = 0, False
            for n, at in ticks:
                c = c + n * (t == at).astype(jnp.int32)
                now = now | (t == at)

            @pl.when(now)
            def _(stage=stages[name], c=c):
                stage(c)

        return 0

    lax.fori_loop(0, TICKS, tick, 0)

    def drain(c, _):
        for copies in (ag1(c), *ag2(c), [cx(c, j) for j in range(3)], rs1(c), rs2(c), gx1(c), gx2(c)):
            for copy in copies:
                copy.wait_send()
        for copies in ([cf(c, i) for i in range(4)], *p1(c), *p2(c)):
            for copy in copies:
                copy.wait_send()
        for copy in final(c):
            copy.wait()
        return 0

    lax.fori_loop(0, N, drain, 0)
    for n, (staged, hbm) in enumerate(((dg, dgate_hbm), (du, dup_hbm), (dd, ddown_hbm))):
        pltpu.make_async_copy(staged, hbm, dw_sem.at[n]).wait()


PIECES = 4


def publish(*refs):
    ins, outs, held, in_sem, out_sem = refs[:5], refs[5:10], refs[10:15], refs[15], refs[16]
    arriving, leaving = [], []
    for i in (2, 3, 4, 0, 1):
        pieces = PIECES if i > 1 else 1
        rows = ins[i].shape[0] // pieces
        for n in range(pieces):
            at = pl.ds(n * rows, rows)
            arriving.append(pltpu.make_async_copy(ins[i].at[at], held[i].at[at], in_sem.at[i, n]))
            leaving.append(pltpu.make_async_copy(held[i].at[at], outs[i].at[at], out_sem.at[i, n]))
    for copy in arriving:
        copy.start()
    for come, go in zip(arriving, leaving):
        come.wait()
        go.start()
    for copy in leaving:
        copy.wait()


def local(dims, tokens, cotangent, gate_weight, up_weight, down_weight, gate_mask, up_mask, down_mask):
    Z, Y, X, N, R = dims
    T = Z * Y * R
    DL, FL = gate_weight.shape
    half, Q = T // 2, T // 2 // X
    H = Q // 2
    smem, hbm = (pl.BlockSpec(memory_space=s) for s in (pltpu.SMEM, pl.ANY))
    far = pl.BlockSpec(memory_space=pltpu.HBM)
    dma = pltpu.SemaphoreType.DMA
    zy = max(Z, Y)
    ax = max(zy - 1, 1)
    results = pl.pallas_call(
        functools.partial(kernel, dims),
        out_shape=(
            jax.ShapeDtypeStruct((N, R, DL), BF16),
            jax.ShapeDtypeStruct((N, R, DL), BF16),
            jax.ShapeDtypeStruct((DL, FL), BF16),
            jax.ShapeDtypeStruct((DL, FL), BF16),
            jax.ShapeDtypeStruct((FL, DL), BF16),
        ),
        in_specs=[hbm, hbm, hbm, hbm, hbm, smem, smem, smem],
        out_specs=(hbm,) * 5,
        scratch_shapes=[
            pltpu.VMEM((DL, FL), BF16),
            pltpu.VMEM((DL, FL), BF16),
            pltpu.VMEM((FL, DL), BF16),
            pltpu.VMEM((2, N, Z, Y, R, DL), BF16),
            pltpu.VMEM((N, 3, T, FL), F32),
            pltpu.VMEM((N, 3, half, FL), F32),
            pltpu.VMEM((N, X, 2, 3, H, FL), BF16),
            pltpu.VMEM((N, 2, 3, H, FL), BF16),
            pltpu.VMEM((N, 2, 3, H, FL), BF16),
            pltpu.VMEM((N, 4, 3, H, FL), BF16),
            pltpu.VMEM((N, 2 * X, 2, 3, H, FL), BF16),
            pltpu.VMEM((N, 2, Z, Y, R, DL), BF16),
            pltpu.VMEM((N, 2, ax, zy, R, DL), BF16),
            pltpu.VMEM((N, 2, zy, R, DL), F32),
            pltpu.VMEM((N, 2, zy, R, DL), BF16),
            pltpu.VMEM((N, 2, ax, R, DL), BF16),
            pltpu.VMEM((2, N, R, DL), BF16),
            pltpu.VMEM((DL, FL), BF16),
            pltpu.VMEM((DL, FL), BF16),
            pltpu.VMEM((FL, DL), BF16),
            dma((2,)),
            dma((2, N)),
            dma((3,)),
            dma((3,)),
            *[dma((N, 2, ax))] * 4,
            *[dma((N, 3))] * 2,
            *[dma((N, 4))] * 2,
            *[dma((N, 2))] * 6,
            *[dma((N, 4))] * 2,
            *[dma((N, 2, ax))] * 4,
        ],
        compiler_params=pltpu.CompilerParams(
            collective_id=0, has_side_effects=True, vmem_limit_bytes=60 * 2**20
        ),
    )(tokens.reshape(N, R, DL), cotangent.reshape(N, R, DL), gate_weight, up_weight, down_weight, gate_mask, up_mask, down_mask)
    shared = pl.pallas_call(
        publish,
        out_shape=tuple(jax.ShapeDtypeStruct(r.shape, r.dtype) for r in results),
        in_specs=[far] * 5,
        out_specs=(far,) * 5,
        scratch_shapes=[*[pltpu.VMEM(r.shape, r.dtype) for r in results], dma((5, PIECES)), dma((5, PIECES))],
        compiler_params=pltpu.CompilerParams(vmem_limit_bytes=60 * 2**20),
    )(*results)
    return (shared[0].reshape(tokens.shape), shared[1].reshape(tokens.shape), *shared[2:])


def solution(mesh, dims=(4, 4, 4, 4, 16)):
    return jax.shard_map(
        functools.partial(local, dims),
        mesh=mesh,
        in_specs=(
            P("row", "col"),
            P("row", "col"),
            P("col", "row"),
            P("col", "row"),
            P("row", "col"),
            P("col", "row"),
            P("col", "row"),
            P("row", "col"),
        ),
        out_specs=(
            P("row", "col"),
            P("row", "col"),
            P("col", "row"),
            P("col", "row"),
            P("row", "col"),
        ),
        check_vma=False,
    )
```

time: 118 us -> 103 us (0.87)
  local copies, waits for them, and re-layouts: 9.53 us -> 0 us
  Pallas kernels: 107 us -> 102 us
    pallas_call x1, Pallas kernels: 107 us -> 96.5 us  [local(): pl.pallas_call(functools.partial(kernel, dims), out_shape=(jax.ShapeDtype...]
    unnamed x9 -> x0, local copies, waits for them, and re-layouts: 9.53 us -> none
    pallas_call x0 -> x1, Pallas kernels: none -> 5.26 us  [local(): pl.pallas_call(publish, out_shape=tuple((jax.ShapeDtypeStruct(r.shape, r....]
where the time goes in v2:
time: 103 us; the launch traced here: 102 us
  Pallas kernels  102 us (99%)
    pallas_call x1, Pallas kernels, local(): pl.pallas_call(functools.partial(kernel, dims), out_shape=(jax.ShapeDtype...  96.5 us
    pallas_call x1, Pallas kernels, local(): pl.pallas_call(publish, out_shape=tuple((jax.ShapeDtypeStruct(r.shape, r....  5.26 us

profile of v2, /device:TPU:0, one launch (start us, length us, event | category | flops | bytes accessed | tf_op | source)
XLA Modules:
  0.0 102.4 jit_solution(1170681826590989715)
XLA Ops:
  0.6 96.5 %shard_map.119 = (bf16[4,16,1024]{2,1,0:T(8,128)(2,1)}, bf16[4,16,1024]{2,1,0:T(8,128)(2,1)}, bf16[1024,896]{1,0:T(8,128)(2,1)}, bf16[1024,896]{1,0:T(8,128)(2,1)}, bf16[896,1024]{1,0:T(8,128)(2,1)}) custom-call(bf16[4,16,1024]{2,1,0:T(8,128)(2,1)} %bitcast.4, bf16[4,16,1024]{2,1,0:T(8,128)(2,1)} %bitcast.5, bf16[1024,896]{1,0:T(8,128)(2,1)} %gate_hbm.1, ...), custom_call_target="tpu_custom_call" | custom-call | tf_op jit(solution)/shard_map/pallas_call | solution.py:429
  97.2 5.3 %shard_map.120 = (bf16[4,16,1024]{2,1,0:T(8,128)(2,1)}, bf16[4,16,1024]{2,1,0:T(8,128)(2,1)}, bf16[1024,896]{1,0:T(8,128)(2,1)}, bf16[1024,896]{1,0:T(8,128)(2,1)}, bf16[896,1024]{1,0:T(8,128)(2,1)}) custom-call(bf16[4,16,1024]{2,1,0:T(8,128)(2,1)} %get-tuple-element.15.refs_0_, bf16[4,16,1024]{2,1,0:T(8,128)(2,1)} %get-tuple-element.16.refs_1_, ...), custom_call_target="tpu_custom_call" | custom-call | tf_op jit(solution)/shard_map/pallas_call | solution.py:476

commit v3 on v2

v3 whole, which is shorter than its diff:
```python
import functools

import jax
import jax.numpy as jnp
from jax import lax
from jax.experimental import pallas as pl
from jax.experimental.pallas import tpu as pltpu
from jax.sharding import PartitionSpec as P

BLOCK = 128
MESH = pl.DeviceIdType.MESH
F32 = jnp.float32
BF16 = jnp.bfloat16

ORDER = (
    ("forward", 0, 0, (1, 4, 8, 9)),
    ("relay", 0, 0, (4, 7, 11, 13)),
    ("pass_on", 0, 0, (9, 14, 17, 19)),
    ("backward", 0, 0, (12, 14, 19, 20)),
    ("gate_grads", 1, 0, (23,)),
    ("forward", 1, 0, (2, 5, 7, 10)),
    ("down_grads", 1, 0, (20,)),
    ("gather", 0, 1, (0, 2, 3)),
    ("share", 1, 0, (3, 6, 8, 11)),
    ("narrow", 1, 0, (14, 15, 24, 25)),
    ("backward", 1, 0, (10, 13, 21, 22)),
    ("up_grads", 1, 0, (22,)),
    ("gather_on", 1, 0, (0, 2, 5, 6)),
    ("relay", 1, 0, (5, 7, 9, 13)),
    ("spread", 1, 0, (8, 10, 16, 18)),
    ("gate_grads", 0, 0, (22,)),
    ("spread", 0, 0, (8, 11, 14, 15)),
    ("activate", None, 0, (6, 8, 13, 14)),
    ("share", 0, 0, (2, 5, 8, 10)),
    ("gather_on", 0, 1, (1, 5, 7)),
    ("settle", None, 0, (8, 11, 14, 17)),
    ("down_grads", 0, 0, (22,)),
    ("narrow", 0, 0, (14, 16, 22, 23)),
    ("pass_on", 1, 0, (8, 12, 19, 20)),
    ("settle_on", None, 0, (12, 14, 25, 27)),
    ("gather", 1, 1, (0, 2, 4)),
    ("finish", 0, 0, (17, 19, 25, 26)),
    ("finish", 1, 0, (17, 18, 26, 27)),
    ("up_grads", 0, 0, (24,)),
)
TICKS = 28


def column_tiles(width):
    return [(at, min(256, width - at)) for at in range(0, width, 256)]


def kernel(
    dims,
    tok_hbm, cot_hbm, gate_hbm, up_hbm, down_hbm, gate_mask, up_mask, down_mask,
    out_hbm, grad_hbm, dgate_hbm, dup_hbm, ddown_hbm,
    wg, wu, wd, act, part, rpart, xs, xq, xt, xr, hall, outp, r1, r2f, r2s, r2r, fin, dg, du, dd,
    own_sem, o_sem, w_sem, dw_sem, ag1_s, ag1_r, ag2_s, ag2_r, cx_s, cx_r, rs1_s, rs1_r, rs2_s, rs2_r, gx1_s, gx1_r, gx2_s, gx2_r, cf_s, cf_r,
    p1_s, p1_r, p2_s, p2_r,
):
    Z, Y, X, N, R = dims
    T = Z * Y * R
    half = T // 2
    Q = half // X
    H = Q // 2
    DL, FL = wg.shape
    DH = DL // 2
    columns = (slice(0, DH), slice(DH, DL))
    row = lax.axis_index("row")
    col = lax.axis_index("col")
    z, y = row // Y, row % Y
    x, k = col // 2, col % 2

    def at_z(d):
        return (((z + d) % Z) * Y + y, col)

    def at_y(d):
        return (z * Y + (y + d) % Y, col)

    def at_x(d):
        return (row, ((x + d) % X) * 2 + k)

    other = (row, x * 2 + 1 - k)

    def remote(src, dst, ssem, rsem, where):
        return pltpu.make_async_remote_copy(
            src_ref=src, dst_ref=dst, send_sem=ssem, recv_sem=rsem, device_id=where, device_id_type=MESH
        )

    def ag1(c, g):
        return [
            remote(
                (tok_hbm, cot_hbm)[g].at[c, :, columns[h]], act.at[g, c, z, y, :, columns[h]],
                ag1_s.at[c, g, h, d - 1], ag1_r.at[c, g, h, d - 1], (at_y, at_z)[h](d),
            )
            for h, size in ((0, Y), (1, Z))
            for d in range(1, size)
        ]

    def ag2(c, g):
        pieces = (act.at[g, c, z, :, :, columns[0]], act.at[g, c, :, y, :, columns[1]])
        return [
            remote(pieces[h], pieces[h], ag2_s.at[c, g, h, d - 1], ag2_r.at[c, g, h, d - 1], (at_z, at_y)[h](d))
            for h, size in ((0, Z), (1, Y))
            for d in range(1, size)
        ]

    def cx(c, j):
        return remote(
            part.at[c, j, pl.ds((1 - k) * half, half)], rpart.at[c, j], cx_s.at[c, j], cx_r.at[c, j], other
        )

    def rs1(c, g):
        js = slice(0, 2) if g == 0 else slice(2, 3)
        right, left, far = (x + 1) % X, (x + X - 1) % X, (x + 2) % X
        moves = (
            (xs.at[c, far, 0, js], xq.at[c, 0, js], 1),
            (xs.at[c, far, 1, js], xq.at[c, 1, js], X - 1),
            (xs.at[c, right, 1, js], xr.at[c, 0, js], 1),
            (xs.at[c, left, 0, js], xr.at[c, 1, js], X - 1),
        )
        return [
            remote(src, dst, rs1_s.at[c, g, i], rs1_r.at[c, g, i], at_x(d)) for i, (src, dst, d) in enumerate(moves)
        ]

    def rs2(c, g):
        js = slice(0, 2) if g == 0 else slice(2, 3)
        return [
            remote(xt.at[c, i, js], xr.at[c, 2 + i, js], rs2_s.at[c, g, i], rs2_r.at[c, g, i], at_x(d))
            for i, d in ((0, 1), (1, X - 1))
        ]

    def gx1(c, g):
        js = slice(0, 1) if g == 0 else slice(1, 3)
        mine = hall.at[c, k * X + x, :, js]
        return [remote(mine, mine, gx1_s.at[c, g, i], gx1_r.at[c, g, i], at_x(d)) for i, d in ((0, 1), (1, X - 1))]

    def gx2(c, g):
        js = slice(0, 1) if g == 0 else slice(1, 3)
        pieces = [hall.at[c, k * X + (x + X - d) % X, i, js] for i, d in ((0, 1), (1, X - 1))]
        return [
            remote(pieces[i], pieces[i], gx2_s.at[c, g, i], gx2_r.at[c, g, i], at_x(d)) for i, d in ((0, 1), (1, X - 1))
        ]

    def cf(c, g, i):
        js = slice(0, 1) if g == 0 else slice(1, 3)
        block = hall.at[c, k * X + (x + (0, X - 1, 1, 2)[i]) % X, :, js]
        return remote(block, block, cf_s.at[c, g, i], cf_r.at[c, g, i], other)

    def p1(c, g, h):
        size, at = ((Z, at_z), (Y, at_y))[h]
        copies = []
        for d in range(1, size):
            piece = (outp.at[c, g, (z + d) % Z, :, :, columns[0]], outp.at[c, g, :, (y + d) % Y, :, columns[1]])[h]
            copies.append(remote(piece, r1.at[c, g, h, d - 1], p1_s.at[c, g, h, d - 1], p1_r.at[c, g, h, d - 1], at(d)))
        return copies

    def p2(c, g, h):
        size, at, me = ((Y, at_y, y), (Z, at_z, z))[h]
        return [
            remote(
                r2s.at[c, g, h, (me + d) % size], r2r.at[c, g, h, d - 1],
                p2_s.at[c, g, h, d - 1], p2_r.at[c, g, h, d - 1], at(d),
            )
            for d in range(1, size)
        ]

    def start(copies):
        for copy in copies:
            copy.start()

    def recv(copies):
        for copy in copies:
            copy.wait_recv()

    loads = [
        pltpu.make_async_copy(src, dst, w_sem.at[i])
        for i, (src, dst) in enumerate(((gate_hbm, wg), (up_hbm, wu), (down_hbm, wd)))
    ]
    own = [
        pltpu.make_async_copy(src, act.at[i, :, z, y], own_sem.at[i]) for i, src in enumerate((tok_hbm, cot_hbm))
    ]
    start(own)
    start(loads)
    peers = [other] + [at_x(d) for d in (1, X - 1)] + [at_y(d) for d in range(1, Y)] + [at_z(d) for d in range(1, Z)]
    barrier = pltpu.get_barrier_semaphore()
    for peer in peers:
        pl.semaphore_signal(barrier, inc=1, device_id=peer, device_id_type=MESH)
    pl.semaphore_wait(barrier, len(peers))

    def gather(c, g):
        start(ag1(c, g))

    def gather_on(c, g):
        recv(ag1(c, g))
        start(ag2(c, g))

    gather(0, 0)
    gather(0, 1)
    for copy in own:
        copy.wait()
    gather_on(0, 0)

    for copy, weight, mask in zip(loads, (wg, wu, wd), (gate_mask, up_mask, down_mask)):
        copy.wait()
        high, wide = weight.shape[0] // BLOCK, weight.shape[1] // BLOCK

        def keep_row(i, _, weight=weight, mask=mask, wide=wide):
            rows = pl.ds(pl.multiple_of(i * BLOCK, BLOCK), BLOCK)
            for j in range(wide):
                cols = slice(j * BLOCK, (j + 1) * BLOCK)
                kept = jnp.full((BLOCK, BLOCK), mask[i, j], jnp.int32).astype(F32).astype(BF16)
                weight[rows, cols] = weight[rows, cols] * kept
            return 0

        lax.fori_loop(0, high, keep_row, 0)

    def forward(c, g):
        recv(ag2(c, g))
        features = act[g, c].reshape(T, DL)
        for j in (0, 1) if g == 0 else (2,):
            for at, width in column_tiles(FL):
                if j < 2:
                    weight, sums = (wg, wu)[j][:, at : at + width], (((1,), (0,)), ((), ()))
                else:
                    weight, sums = wd[at : at + width, :], (((1,), (1,)), ((), ()))
                part[c, j, :, at : at + width] = lax.dot_general(features, weight, sums, preferred_element_type=F32)
            cx(c, j).start()

    def mine(c, j, b, h):
        at = pl.multiple_of(b * Q + h * H, H)
        here = pl.ds(pl.multiple_of(k * half + at, H), H)
        return part[c, j, here, :] + rpart[c, j, pl.ds(at, H), :]

    def share(c, g):
        for j in (0, 1) if g == 0 else (2,):
            cx(c, j).wait_recv()
            for b in range(X):
                for h in range(2):
                    xs[c, b, h, j] = mine(c, j, b, h).astype(BF16)
        start(rs1(c, g))

    def relay(c, g):
        arriving, onward = rs1(c, g), rs2(c, g)
        for i, d in ((0, 1), (1, X - 1)):
            arriving[i].wait_recv()
            for j in (0, 1) if g == 0 else (2,):
                xt[c, i, j] = (mine(c, j, (x + d) % X, i) + xq[c, i, j].astype(F32)).astype(BF16)
            onward[i].start()

    def activate(c):
        for g in range(2):
            recv(rs1(c, g)[2:])
            recv(rs2(c, g))
        block = k * X + x
        for h in range(2):

            def total(j, h=h):
                return mine(c, j, x, h) + xr[c, 1 - h, j].astype(F32) + xr[c, 2 + h, j].astype(F32)

            gate, up, back = total(0), total(1), total(2)
            s = 1.0 / (1.0 + jnp.exp(-gate))
            hall[c, block, h, 0] = (gate * s * up).astype(BF16)
            hall[c, block, h, 1] = (back * up * s * (1.0 + gate * (1.0 - s))).astype(BF16)
            hall[c, block, h, 2] = (back * gate * s).astype(BF16)
        for g in range(2):
            start(gx1(c, g))
            cf(c, g, 0).start()

    def spread(c, g):
        for i, (arriving, onward) in enumerate(zip(gx1(c, g), gx2(c, g))):
            arriving.wait_recv()
            onward.start()
            cf(c, g, 1 + i).start()

    def pass_on(c, g):
        recv(gx2(c, g))
        cf(c, g, 3).start()

    def backward(c, g):
        for i in range(4):
            cf(c, g, i).wait_recv()
        terms = ((0, wd),) if g == 0 else ((1, wg), (2, wu))
        for h in range(2):
            for at, width in column_tiles(DH):
                cols = slice(h * DH + at, h * DH + at + width)
                value = 0.0
                for j, weight in terms:
                    left = hall[c, :, :, j].reshape(T, FL)
                    if g == 0:
                        value += jnp.dot(left, weight[:, cols], preferred_element_type=F32)
                    else:
                        value += lax.dot_general(
                            left, weight[cols, :], (((1,), (1,)), ((), ())), preferred_element_type=F32
                        )
                outp[c, g, :, :, :, cols] = value.astype(BF16).reshape(Z, Y, R, width)
            start(p1(c, g, h))

    def narrow(c, g):
        for h, size, count in ((0, Z, Y), (1, Y, Z)):
            recv(p1(c, g, h))
            for b in range(count):
                value = (outp[c, g, z, b, :, columns[0]], outp[c, g, b, y, :, columns[1]])[h].astype(F32)
                for d in range(1, size):
                    value = value + r1[c, g, h, d - 1, b].astype(F32)
                r2f[c, g, h, b] = value
                r2s[c, g, h, b] = value.astype(BF16)
            start(p2(c, g, h))

    def final(c, g):
        return pltpu.make_async_copy(fin.at[g, c], (out_hbm, grad_hbm)[g].at[c], o_sem.at[g, c])

    def finish(c, g):
        for h, size, me in ((0, Y, y), (1, Z, z)):
            recv(p2(c, g, h))
            value = r2f[c, g, h, me]
            for d in range(1, size):
                value = value + r2r[c, g, h, d - 1].astype(F32)
            fin[g, c, :, columns[h]] = value.astype(BF16)
        final(c, g).start()

    def weight_write(staged, hbm, n, part_of):
        rows = slice(0, 512) if part_of == 0 else slice(512, staged.shape[0])
        return pltpu.make_async_copy(staged.at[rows], hbm.at[rows], dw_sem.at[n, part_of])

    def weight_grad(staged, lhs, rhs, mask, hbm, n, part_of):
        high, wide = staged.shape
        for top, tall in column_tiles(high)[2 * part_of : 2 * part_of + 2]:
            left = lhs(top, tall)
            for at, width in column_tiles(wide):
                value = lax.dot_general(left, rhs(at, width), (((0,), (0,)), ((), ())), preferred_element_type=F32)
                for a in range(0, tall, BLOCK):
                    for b in range(0, width, BLOCK):
                        kept = jnp.full((BLOCK, BLOCK), mask[(top + a) // BLOCK, (at + b) // BLOCK], jnp.int32).astype(F32)
                        staged[top + a : top + a + BLOCK, at + b : at + b + BLOCK] = (
                            value[a : a + BLOCK, b : b + BLOCK] * kept
                        ).astype(BF16)
        weight_write(staged, hbm, n, part_of).start()

    everything = N * T

    def grads_of(j):
        return lambda at, width: hall[:, :, :, j, :, at : at + width].reshape(everything, width)

    def tokens_of(at, width):
        return act[0, :, :, :, :, at : at + width].reshape(everything, width)

    def upstream_of(at, width):
        return act[1, :, :, :, :, at : at + width].reshape(everything, width)

    def gate_grads(_, part_of):
        weight_grad(dg, tokens_of, grads_of(1), gate_mask, dgate_hbm, 0, part_of)

    def up_grads(_, part_of):
        weight_grad(du, tokens_of, grads_of(2), up_mask, dup_hbm, 1, part_of)

    def down_grads(_, part_of):
        weight_grad(dd, grads_of(0), upstream_of, down_mask, ddown_hbm, 2, part_of)

    def sent(copies):
        for copy in copies:
            copy.wait_send()

    def settle(c):
        for g in range(2):
            sent(ag1(c, g) + ag2(c, g) + rs1(c, g) + rs2(c, g))
        sent([cx(c, j) for j in range(3)])

    def settle_on(c):
        for g in range(2):
            sent(gx1(c, g) + gx2(c, g) + [cf(c, g, i) for i in range(4)] + p1(c, g, 0) + p1(c, g, 1))

    stages = {
        "gather": gather, "gather_on": gather_on, "forward": forward, "share": share, "relay": relay,
        "activate": activate, "spread": spread, "pass_on": pass_on, "backward": backward, "narrow": narrow,
        "finish": finish, "gate_grads": gate_grads, "up_grads": up_grads, "down_grads": down_grads,
        "settle": settle, "settle_on": settle_on,
    }

    def tick(t, _):
        for name, group, first, ticks in ORDER:
            now = False
            for at in ticks:
                now = now | (t == at)

            @pl.when(now)
            def _(stage=stages[name], group=group, first=first, ticks=ticks):
                c = first
                for at in ticks[1:]:
                    c = c + (t >= at).astype(jnp.int32)
                if group is None:
                    stage(c)
                else:
                    stage(c, group)

        return 0

    lax.fori_loop(0, TICKS, tick, 0)

    def drain(c, _):
        for g in range(2):
            for h in range(2):
                sent(p2(c, g, h))
            final(c, g).wait()
        return 0

    lax.fori_loop(0, N, drain, 0)
    for n, (staged, hbm) in enumerate(((dg, dgate_hbm), (du, dup_hbm), (dd, ddown_hbm))):
        for part_of in range(2):
            weight_write(staged, hbm, n, part_of).wait()


PIECES = 4


def publish(*refs):
    ins, outs, held, in_sem, out_sem = refs[:5], refs[5:10], refs[10:15], refs[15], refs[16]
    arriving, leaving = [], []
    for i in (2, 3, 4, 0, 1):
        pieces = PIECES if i > 1 else 1
        rows = ins[i].shape[0] // pieces
        for n in range(pieces):
            at = pl.ds(n * rows, rows)
            arriving.append(pltpu.make_async_copy(ins[i].at[at], held[i].at[at], in_sem.at[i, n]))
            leaving.append(pltpu.make_async_copy(held[i].at[at], outs[i].at[at], out_sem.at[i, n]))
    for copy in arriving:
        copy.start()
    for come, go in zip(arriving, leaving):
        come.wait()
        go.start()
    for copy in leaving:
        copy.wait()


def local(dims, tokens, cotangent, gate_weight, up_weight, down_weight, gate_mask, up_mask, down_mask):
    Z, Y, X, N, R = dims
    T = Z * Y * R
    DL, FL = gate_weight.shape
    half, Q = T // 2, T // 2 // X
    H = Q // 2
    smem, hbm = (pl.BlockSpec(memory_space=s) for s in (pltpu.SMEM, pl.ANY))
    far = pl.BlockSpec(memory_space=pltpu.HBM)
    dma = pltpu.SemaphoreType.DMA
    zy = max(Z, Y)
    ax = max(zy - 1, 1)
    results = pl.pallas_call(
        functools.partial(kernel, dims),
        out_shape=(
            jax.ShapeDtypeStruct((N, R, DL), BF16),
            jax.ShapeDtypeStruct((N, R, DL), BF16),
            jax.ShapeDtypeStruct((DL, FL), BF16),
            jax.ShapeDtypeStruct((DL, FL), BF16),
            jax.ShapeDtypeStruct((FL, DL), BF16),
        ),
        in_specs=[hbm, hbm, hbm, hbm, hbm, smem, smem, smem],
        out_specs=(hbm,) * 5,
        scratch_shapes=[
            pltpu.VMEM((DL, FL), BF16),
            pltpu.VMEM((DL, FL), BF16),
            pltpu.VMEM((FL, DL), BF16),
            pltpu.VMEM((2, N, Z, Y, R, DL), BF16),
            pltpu.VMEM((N, 3, T, FL), F32),
            pltpu.VMEM((N, 3, half, FL), F32),
            pltpu.VMEM((N, X, 2, 3, H, FL), BF16),
            pltpu.VMEM((N, 2, 3, H, FL), BF16),
            pltpu.VMEM((N, 2, 3, H, FL), BF16),
            pltpu.VMEM((N, 4, 3, H, FL), BF16),
            pltpu.VMEM((N, 2 * X, 2, 3, H, FL), BF16),
            pltpu.VMEM((N, 2, Z, Y, R, DL), BF16),
            pltpu.VMEM((N, 2, 2, ax, zy, R, DL // 2), BF16),
            pltpu.VMEM((N, 2, 2, zy, R, DL // 2), F32),
            pltpu.VMEM((N, 2, 2, zy, R, DL // 2), BF16),
            pltpu.VMEM((N, 2, 2, ax, R, DL // 2), BF16),
            pltpu.VMEM((2, N, R, DL), BF16),
            pltpu.VMEM((DL, FL), BF16),
            pltpu.VMEM((DL, FL), BF16),
            pltpu.VMEM((FL, DL), BF16),
            dma((2,)),
            dma((2, N)),
            dma((3,)),
            dma((3, 2)),
            *[dma((N, 2, 2, ax))] * 4,
            *[dma((N, 3))] * 2,
            *[dma((N, 2, 4))] * 2,
            *[dma((N, 2, 2))] * 6,
            *[dma((N, 2, 4))] * 2,
            *[dma((N, 2, 2, ax))] * 4,
        ],
        compiler_params=pltpu.CompilerParams(
            collective_id=0, has_side_effects=True, vmem_limit_bytes=60 * 2**20
        ),
    )(tokens.reshape(N, R, DL), cotangent.reshape(N, R, DL), gate_weight, up_weight, down_weight, gate_mask, up_mask, down_mask)
    shared = pl.pallas_call(
        publish,
        out_shape=tuple(jax.ShapeDtypeStruct(r.shape, r.dtype) for r in results),
        in_specs=[far] * 5,
        out_specs=(far,) * 5,
        scratch_shapes=[*[pltpu.VMEM(r.shape, r.dtype) for r in results], dma((5, PIECES)), dma((5, PIECES))],
        compiler_params=pltpu.CompilerParams(vmem_limit_bytes=60 * 2**20),
    )(*results)
    return (shared[0].reshape(tokens.shape), shared[1].reshape(tokens.shape), *shared[2:])


def solution(mesh, dims=(4, 4, 4, 4, 16)):
    return jax.shard_map(
        functools.partial(local, dims),
        mesh=mesh,
        in_specs=(
            P("row", "col"),
            P("row", "col"),
            P("col", "row"),
            P("col", "row"),
            P("row", "col"),
            P("col", "row"),
            P("col", "row"),
            P("row", "col"),
        ),
        out_specs=(
            P("row", "col"),
            P("row", "col"),
            P("col", "row"),
            P("col", "row"),
            P("row", "col"),
        ),
        check_vma=False,
    )
```

time: 103 us -> 100 us (0.971)
  Pallas kernels: 102 us -> 99.3 us
    pallas_call x1, Pallas kernels: 96.5 us -> 94 us  [local(): pl.pallas_call(functools.partial(kernel, dims), out_shape=(jax.ShapeDtype...]
where the time goes in v3:
time: 100 us; the launch traced here: 99.9 us
  Pallas kernels  99.3 us (99%)
    pallas_call x1, Pallas kernels, local(): pl.pallas_call(functools.partial(kernel, dims), out_shape=(jax.ShapeDtype...  94 us
    pallas_call x1, Pallas kernels, local(): pl.pallas_call(publish, out_shape=tuple((jax.ShapeDtypeStruct(r.shape, r....  5.26 us

profile of v3, /device:TPU:0, one launch (start us, length us, event | category | flops | bytes accessed | tf_op | source)
XLA Modules:
  0.0 99.9 jit_solution(8156881579650120278)
XLA Ops:
  0.6 94.0 %shard_map.119 = (bf16[4,16,1024]{2,1,0:T(8,128)(2,1)}, bf16[4,16,1024]{2,1,0:T(8,128)(2,1)}, bf16[1024,896]{1,0:T(8,128)(2,1)}, bf16[1024,896]{1,0:T(8,128)(2,1)}, bf16[896,1024]{1,0:T(8,128)(2,1)}) custom-call(bf16[4,16,1024]{2,1,0:T(8,128)(2,1)} %bitcast.4, bf16[4,16,1024]{2,1,0:T(8,128)(2,1)} %bitcast.5, bf16[1024,896]{1,0:T(8,128)(2,1)} %gate_hbm.1, ...), custom_call_target="tpu_custom_call" | custom-call | tf_op jit(solution)/shard_map/pallas_call | solution.py:446
  94.7 5.3 %shard_map.120 = (bf16[4,16,1024]{2,1,0:T(8,128)(2,1)}, bf16[4,16,1024]{2,1,0:T(8,128)(2,1)}, bf16[1024,896]{1,0:T(8,128)(2,1)}, bf16[1024,896]{1,0:T(8,128)(2,1)}, bf16[896,1024]{1,0:T(8,128)(2,1)}) custom-call(bf16[4,16,1024]{2,1,0:T(8,128)(2,1)} %get-tuple-element.15.refs_0_, bf16[4,16,1024]{2,1,0:T(8,128)(2,1)} %get-tuple-element.16.refs_1_, ...), custom_call_target="tpu_custom_call" | custom-call | tf_op jit(solution)/shard_map/pallas_call | solution.py:493

commit v4 on v3

--- a/solution.py
+++ b/solution.py
@@ -13,37 +13,37 @@
 BF16 = jnp.bfloat16
 
 ORDER = (
-    ("forward", 0, 0, (1, 4, 8, 9)),
-    ("relay", 0, 0, (4, 7, 11, 13)),
-    ("pass_on", 0, 0, (9, 14, 17, 19)),
+    ("gather_on", 1, 0, (1, 2, 4, 6)),
+    ("settle", None, 0, (9, 12, 16, 17)),
+    ("spread", 0, 0, (10, 12, 15, 16)),
+    ("gate_grads", 1, 0, (23,)),
+    ("share", 1, 0, (2, 4, 10, 11)),
+    ("up_grads", 0, 0, (22,)),
+    ("spread", 1, 0, (9, 12, 15, 17)),
+    ("gather", 1, 1, (1, 2, 3)),
+    ("gather", 0, 1, (0, 1, 2)),
+    ("down_grads", 1, 0, (22,)),
+    ("narrow", 0, 0, (14, 18, 22, 23)),
+    ("forward", 0, 0, (1, 3, 5, 10)),
     ("backward", 0, 0, (12, 14, 19, 20)),
-    ("gate_grads", 1, 0, (23,)),
-    ("forward", 1, 0, (2, 5, 7, 10)),
-    ("down_grads", 1, 0, (20,)),
-    ("gather", 0, 1, (0, 2, 3)),
-    ("share", 1, 0, (3, 6, 8, 11)),
-    ("narrow", 1, 0, (14, 15, 24, 25)),
-    ("backward", 1, 0, (10, 13, 21, 22)),
-    ("up_grads", 1, 0, (22,)),
-    ("gather_on", 1, 0, (0, 2, 5, 6)),
-    ("relay", 1, 0, (5, 7, 9, 13)),
-    ("spread", 1, 0, (8, 10, 16, 18)),
+    ("relay", 0, 0, (3, 7, 11, 12)),
+    ("gather_on", 0, 1, (1, 3, 4)),
+    ("pass_on", 0, 0, (11, 13, 17, 19)),
+    ("narrow", 1, 0, (13, 18, 24, 25)),
+    ("down_grads", 0, 0, (25,)),
     ("gate_grads", 0, 0, (22,)),
-    ("spread", 0, 0, (8, 11, 14, 15)),
-    ("activate", None, 0, (6, 8, 13, 14)),
-    ("share", 0, 0, (2, 5, 8, 10)),
-    ("gather_on", 0, 1, (1, 5, 7)),
-    ("settle", None, 0, (8, 11, 14, 17)),
-    ("down_grads", 0, 0, (22,)),
-    ("narrow", 0, 0, (14, 16, 22, 23)),
-    ("pass_on", 1, 0, (8, 12, 19, 20)),
-    ("settle_on", None, 0, (12, 14, 25, 27)),
-    ("gather", 1, 1, (0, 2, 4)),
-    ("finish", 0, 0, (17, 19, 25, 26)),
-    ("finish", 1, 0, (17, 18, 26, 27)),
-    ("up_grads", 0, 0, (24,)),
+    ("up_grads", 1, 0, (25,)),
+    ("relay", 1, 0, (3, 6, 11, 12)),
+    ("forward", 1, 0, (1, 3, 8, 10)),
+    ("settle_on", None, 0, (12, 19, 24, 25)),
+    ("activate", None, 0, (4, 10, 12, 14)),
+    ("pass_on", 1, 0, (10, 13, 18, 20)),
+    ("share", 0, 0, (1, 3, 7, 10)),
+    ("backward", 1, 0, (10, 14, 20, 21)),
+    ("finish", 0, 0, (18, 23, 25, 26)),
+    ("finish", 1, 0, (17, 21, 25, 26)),
 )
-TICKS = 28
+TICKS = 27
 
 
 def column_tiles(width):

time: 100 us -> 99.2 us (level)
  Pallas kernels: 99.3 us -> 98.3 us
where the time goes in v4:
time: 99.2 us; the launch traced here: 99 us
  Pallas kernels  98.3 us (99%)
    pallas_call x1, Pallas kernels, local(): pl.pallas_call(functools.partial(kernel, dims), out_shape=(jax.ShapeDtype...  93.1 us
    pallas_call x1, Pallas kernels, local(): pl.pallas_call(publish, out_shape=tuple((jax.ShapeDtypeStruct(r.shape, r....  5.26 us

profile of v4, /device:TPU:0, one launch (start us, length us, event | category | flops | bytes accessed | tf_op | source)
XLA Modules:
  0.0 99.0 jit_solution(10787637703123872782)
XLA Ops:
  0.6 93.1 %shard_map.119 = (bf16[4,16,1024]{2,1,0:T(8,128)(2,1)}, bf16[4,16,1024]{2,1,0:T(8,128)(2,1)}, bf16[1024,896]{1,0:T(8,128)(2,1)}, bf16[1024,896]{1,0:T(8,128)(2,1)}, bf16[896,1024]{1,0:T(8,128)(2,1)}) custom-call(bf16[4,16,1024]{2,1,0:T(8,128)(2,1)} %bitcast.4, bf16[4,16,1024]{2,1,0:T(8,128)(2,1)} %bitcast.5, bf16[1024,896]{1,0:T(8,128)(2,1)} %gate_hbm.1, ...), custom_call_target="tpu_custom_call" | custom-call | tf_op jit(solution)/shard_map/pallas_call | solution.py:446
  93.7 5.3 %shard_map.120 = (bf16[4,16,1024]{2,1,0:T(8,128)(2,1)}, bf16[4,16,1024]{2,1,0:T(8,128)(2,1)}, bf16[1024,896]{1,0:T(8,128)(2,1)}, bf16[1024,896]{1,0:T(8,128)(2,1)}, bf16[896,1024]{1,0:T(8,128)(2,1)}) custom-call(bf16[4,16,1024]{2,1,0:T(8,128)(2,1)} %get-tuple-element.15.refs_0_, bf16[4,16,1024]{2,1,0:T(8,128)(2,1)} %get-tuple-element.16.refs_1_, ...), custom_call_target="tpu_custom_call" | custom-call | tf_op jit(solution)/shard_map/pallas_call | solution.py:493

commit v5 on v4

--- a/solution.py
+++ b/solution.py
@@ -91,7 +91,7 @@
         return [
             remote(
                 (tok_hbm, cot_hbm)[g].at[c, :, columns[h]], act.at[g, c, z, y, :, columns[h]],
-                ag1_s.at[c, g, h, d - 1], ag1_r.at[c, g, h, d - 1], (at_y, at_z)[h](d),
+                ag1_s.at[c, g], ag1_r.at[c, g], (at_y, at_z)[h](d),
             )
             for h, size in ((0, Y), (1, Z))
             for d in range(1, size)
@@ -100,14 +100,14 @@
     def ag2(c, g):
         pieces = (act.at[g, c, z, :, :, columns[0]], act.at[g, c, :, y, :, columns[1]])
         return [
-            remote(pieces[h], pieces[h], ag2_s.at[c, g, h, d - 1], ag2_r.at[c, g, h, d - 1], (at_z, at_y)[h](d))
+            remote(pieces[h], pieces[h], ag2_s.at[c, g], ag2_r.at[c, g], (at_z, at_y)[h](d))
             for h, size in ((0, Z), (1, Y))
             for d in range(1, size)
         ]
 
     def cx(c, j):
         return remote(
-            part.at[c, j, pl.ds((1 - k) * half, half)], rpart.at[c, j], cx_s.at[c, j], cx_r.at[c, j], other
+            part.at[c, j, pl.ds((1 - k) * half, half)], rpart.at[c, j], cx_s.at[c], cx_r.at[c, j], other
         )
 
     def rs1(c, g):
@@ -120,39 +120,39 @@
             (xs.at[c, left, 0, js], xr.at[c, 1, js], X - 1),
         )
         return [
-            remote(src, dst, rs1_s.at[c, g, i], rs1_r.at[c, g, i], at_x(d)) for i, (src, dst, d) in enumerate(moves)
+            remote(src, dst, rs1_s.at[c, g], rs1_r.at[c, g, i], at_x(d)) for i, (src, dst, d) in enumerate(moves)
         ]
 
     def rs2(c, g):
         js = slice(0, 2) if g == 0 else slice(2, 3)
         return [
-            remote(xt.at[c, i, js], xr.at[c, 2 + i, js], rs2_s.at[c, g, i], rs2_r.at[c, g, i], at_x(d))
+            remote(xt.at[c, i, js], xr.at[c, 2 + i, js], rs2_s.at[c, g], rs2_r.at[c, g, i], at_x(d))
             for i, d in ((0, 1), (1, X - 1))
         ]
 
     def gx1(c, g):
         js = slice(0, 1) if g == 0 else slice(1, 3)
         mine = hall.at[c, k * X + x, :, js]
-        return [remote(mine, mine, gx1_s.at[c, g, i], gx1_r.at[c, g, i], at_x(d)) for i, d in ((0, 1), (1, X - 1))]
+        return [remote(mine, mine, gx1_s.at[c, g], gx1_r.at[c, g, i], at_x(d)) for i, d in ((0, 1), (1, X - 1))]
 
     def gx2(c, g):
         js = slice(0, 1) if g == 0 else slice(1, 3)
         pieces = [hall.at[c, k * X + (x + X - d) % X, i, js] for i, d in ((0, 1), (1, X - 1))]
         return [
-            remote(pieces[i], pieces[i], gx2_s.at[c, g, i], gx2_r.at[c, g, i], at_x(d)) for i, d in ((0, 1), (1, X - 1))
+            remote(pieces[i], pieces[i], gx2_s.at[c, g], gx2_r.at[c, g, i], at_x(d)) for i, d in ((0, 1), (1, X - 1))
         ]
 
     def cf(c, g, i):
         js = slice(0, 1) if g == 0 else slice(1, 3)
         block = hall.at[c, k * X + (x + (0, X - 1, 1, 2)[i]) % X, :, js]
-        return remote(block, block, cf_s.at[c, g, i], cf_r.at[c, g, i], other)
+        return remote(block, block, cf_s.at[c, g], cf_r.at[c, g, i], other)
 
     def p1(c, g, h):
         size, at = ((Z, at_z), (Y, at_y))[h]
         copies = []
         for d in range(1, size):
             piece = (outp.at[c, g, (z + d) % Z, :, :, columns[0]], outp.at[c, g, :, (y + d) % Y, :, columns[1]])[h]
-            copies.append(remote(piece, r1.at[c, g, h, d - 1], p1_s.at[c, g, h, d - 1], p1_r.at[c, g, h, d - 1], at(d)))
+            copies.append(remote(piece, r1.at[c, g, h, d - 1], p1_s.at[c, g, h], p1_r.at[c, g, h], at(d)))
         return copies
 
     def p2(c, g, h):
@@ -160,10 +160,19 @@
         return [
             remote(
                 r2s.at[c, g, h, (me + d) % size], r2r.at[c, g, h, d - 1],
-                p2_s.at[c, g, h, d - 1], p2_r.at[c, g, h, d - 1], at(d),
+                p2_s.at[c, g, h], p2_r.at[c, g, h], at(d),
             )
             for d in range(1, size)
         ]
+
+    def wait(view, sem):
+        pltpu.make_async_copy(view, view, sem).wait()
+
+    def ag1_bytes(c, g):
+        return act.at[g, c, 0, 0:3]
+
+    def ag2_bytes(c, g):
+        return act.at[g, c, 0:3]
 
     def start(copies):
         for copy in copies:
@@ -192,7 +201,7 @@
         start(ag1(c, g))
 
     def gather_on(c, g):
-        recv(ag1(c, g))
+        wait(ag1_bytes(c, g), ag1_r.at[c, g])
         start(ag2(c, g))
 
     gather(0, 0)
@@ -216,7 +225,7 @@
         lax.fori_loop(0, high, keep_row, 0)
 
     def forward(c, g):
-        recv(ag2(c, g))
+        wait(ag2_bytes(c, g), ag2_r.at[c, g])
         features = act[g, c].reshape(T, DL)
         for j in (0, 1) if g == 0 else (2,):
             for at, width in column_tiles(FL):
@@ -298,7 +307,7 @@
 
     def narrow(c, g):
         for h, size, count in ((0, Z, Y), (1, Y, Z)):
-            recv(p1(c, g, h))
+            wait(r1.at[c, g, h], p1_r.at[c, g, h])
             for b in range(count):
                 value = (outp[c, g, z, b, :, columns[0]], outp[c, g, b, y, :, columns[1]])[h].astype(F32)
                 for d in range(1, size):
@@ -312,7 +321,7 @@
 
     def finish(c, g):
         for h, size, me in ((0, Y, y), (1, Z, z)):
-            recv(p2(c, g, h))
+            wait(r2r.at[c, g, h], p2_r.at[c, g, h])
             value = r2f[c, g, h, me]
             for d in range(1, size):
                 value = value + r2r[c, g, h, d - 1].astype(F32)
@@ -357,18 +366,23 @@
     def down_grads(_, part_of):
         weight_grad(dd, grads_of(0), upstream_of, down_mask, ddown_hbm, 2, part_of)
 
-    def sent(copies):
-        for copy in copies:
-            copy.wait_send()
-
     def settle(c):
         for g in range(2):
-            sent(ag1(c, g) + ag2(c, g) + rs1(c, g) + rs2(c, g))
-        sent([cx(c, j) for j in range(3)])
+            js = slice(0, 2) if g == 0 else slice(2, 3)
+            wait(ag1_bytes(c, g), ag1_s.at[c, g])
+            wait(ag2_bytes(c, g), ag2_s.at[c, g])
+            wait(xs.at[c, 0:2, :, js], rs1_s.at[c, g])
+            wait(xt.at[c, :, js], rs2_s.at[c, g])
+        wait(rpart.at[c], cx_s.at[c])
 
     def settle_on(c):
         for g in range(2):
-            sent(gx1(c, g) + gx2(c, g) + [cf(c, g, i) for i in range(4)] + p1(c, g, 0) + p1(c, g, 1))
+            js = slice(0, 1) if g == 0 else slice(1, 3)
+            wait(hall.at[c, 0:2, :, js], gx1_s.at[c, g])
+            wait(hall.at[c, 0, :, js], gx2_s.at[c, g])
+            wait(hall.at[c, 0:4, :, js], cf_s.at[c, g])
+            for h in range(2):
+                wait(r1.at[c, g, h], p1_s.at[c, g, h])
 
     stages = {
         "gather": gather, "gather_on": gather_on, "forward": forward, "share": share, "relay": relay,
@@ -400,7 +414,7 @@
     def drain(c, _):
         for g in range(2):
             for h in range(2):
-                sent(p2(c, g, h))
+                wait(r2r.at[c, g, h], p2_s.at[c, g, h])
             final(c, g).wait()
         return 0
 
@@ -479,12 +493,15 @@
             dma((2, N)),
             dma((3,)),
             dma((3, 2)),
-            *[dma((N, 2, 2, ax))] * 4,
-            *[dma((N, 3))] * 2,
-            *[dma((N, 2, 4))] * 2,
-            *[dma((N, 2, 2))] * 6,
-            *[dma((N, 2, 4))] * 2,
-            *[dma((N, 2, 2, ax))] * 4,
+            *[dma((N, 2))] * 4,
+            dma((N,)),
+            dma((N, 3)),
+            dma((N, 2)),
+            dma((N, 2, 4)),
+            *[dma((N, 2)), dma((N, 2, 2))] * 3,
+            dma((N, 2)),
+            dma((N, 2, 4)),
+            *[dma((N, 2, 2))] * 4,
         ],
         compiler_params=pltpu.CompilerParams(
             collective_id=0, has_side_effects=True, vmem_limit_bytes=60 * 2**20

time: 99.2 us -> 95.8 us (0.966)
  Pallas kernels: 98.3 us -> 95 us
    pallas_call x1, Pallas kernels: 93.1 us -> 89.7 us  [local(): pl.pallas_call(functools.partial(kernel, dims), out_shape=(jax.ShapeDtype...]
where the time goes in v5:
time: 95.8 us; the launch traced here: 95.6 us
  Pallas kernels  95 us (99%)
    pallas_call x1, Pallas kernels, local(): pl.pallas_call(functools.partial(kernel, dims), out_shape=(jax.ShapeDtype...  89.7 us
    pallas_call x1, Pallas kernels, local(): pl.pallas_call(publish, out_shape=tuple((jax.ShapeDtypeStruct(r.shape, r....  5.26 us

profile of v5, /device:TPU:0, one launch (start us, length us, event | category | flops | bytes accessed | tf_op | source)
XLA Modules:
  0.0 95.6 jit_solution(6583960184964087176)
XLA Ops:
  0.6 89.7 %shard_map.119 = (bf16[4,16,1024]{2,1,0:T(8,128)(2,1)}, bf16[4,16,1024]{2,1,0:T(8,128)(2,1)}, bf16[1024,896]{1,0:T(8,128)(2,1)}, bf16[1024,896]{1,0:T(8,128)(2,1)}, bf16[896,1024]{1,0:T(8,128)(2,1)}) custom-call(bf16[4,16,1024]{2,1,0:T(8,128)(2,1)} %bitcast.4, bf16[4,16,1024]{2,1,0:T(8,128)(2,1)} %bitcast.5, bf16[1024,896]{1,0:T(8,128)(2,1)} %gate_hbm.1, ...), custom_call_target="tpu_custom_call" | custom-call | tf_op jit(solution)/shard_map/pallas_call | solution.py:460
  90.4 5.3 %shard_map.120 = (bf16[4,16,1024]{2,1,0:T(8,128)(2,1)}, bf16[4,16,1024]{2,1,0:T(8,128)(2,1)}, bf16[1024,896]{1,0:T(8,128)(2,1)}, bf16[1024,896]{1,0:T(8,128)(2,1)}, bf16[896,1024]{1,0:T(8,128)(2,1)}) custom-call(bf16[4,16,1024]{2,1,0:T(8,128)(2,1)} %get-tuple-element.15.refs_0_, bf16[4,16,1024]{2,1,0:T(8,128)(2,1)} %get-tuple-element.16.refs_1_, ...), custom_call_target="tpu_custom_call" | custom-call | tf_op jit(solution)/shard_map/pallas_call | solution.py:510

commit v6 on v5

--- a/solution.py
+++ b/solution.py
@@ -13,37 +13,37 @@
 BF16 = jnp.bfloat16
 
 ORDER = (
-    ("gather_on", 1, 0, (1, 2, 4, 6)),
-    ("settle", None, 0, (9, 12, 16, 17)),
-    ("spread", 0, 0, (10, 12, 15, 16)),
-    ("gate_grads", 1, 0, (23,)),
-    ("share", 1, 0, (2, 4, 10, 11)),
-    ("up_grads", 0, 0, (22,)),
-    ("spread", 1, 0, (9, 12, 15, 17)),
-    ("gather", 1, 1, (1, 2, 3)),
-    ("gather", 0, 1, (0, 1, 2)),
-    ("down_grads", 1, 0, (22,)),
-    ("narrow", 0, 0, (14, 18, 22, 23)),
-    ("forward", 0, 0, (1, 3, 5, 10)),
-    ("backward", 0, 0, (12, 14, 19, 20)),
-    ("relay", 0, 0, (3, 7, 11, 12)),
-    ("gather_on", 0, 1, (1, 3, 4)),
-    ("pass_on", 0, 0, (11, 13, 17, 19)),
-    ("narrow", 1, 0, (13, 18, 24, 25)),
-    ("down_grads", 0, 0, (25,)),
-    ("gate_grads", 0, 0, (22,)),
+    ("activate", None, 0, (7, 10, 13, 17)),
+    ("gather", 1, 1, (0, 1, 4)),
+    ("forward", 0, 0, (1, 5, 9, 11)),
+    ("gather_on", 0, 1, (1, 6, 9)),
     ("up_grads", 1, 0, (25,)),
-    ("relay", 1, 0, (3, 6, 11, 12)),
-    ("forward", 1, 0, (1, 3, 8, 10)),
-    ("settle_on", None, 0, (12, 19, 24, 25)),
-    ("activate", None, 0, (4, 10, 12, 14)),
-    ("pass_on", 1, 0, (10, 13, 18, 20)),
-    ("share", 0, 0, (1, 3, 7, 10)),
-    ("backward", 1, 0, (10, 14, 20, 21)),
-    ("finish", 0, 0, (18, 23, 25, 26)),
-    ("finish", 1, 0, (17, 21, 25, 26)),
+    ("gather", 0, 1, (0, 3, 4)),
+    ("down_grads", 0, 0, (26,)),
+    ("spread", 0, 0, (9, 12, 16, 22)),
+    ("gather_on", 1, 0, (0, 1, 3, 7)),
+    ("gate_grads", 0, 0, (30,)),
+    ("backward", 0, 0, (12, 15, 22, 24)),
+    ("spread", 1, 0, (9, 14, 16, 22)),
+    ("relay", 0, 0, (5, 8, 11, 13)),
+    ("share", 1, 0, (4, 6, 7, 11)),
+    ("pass_on", 1, 0, (11, 17, 20, 24)),
+    ("forward", 1, 0, (2, 5, 6, 9)),
+    ("settle", None, 0, (10, 20, 21, 22)),
+    ("down_grads", 1, 0, (24,)),
+    ("gate_grads", 1, 0, (25,)),
+    ("relay", 1, 0, (5, 7, 10, 13)),
+    ("share", 0, 0, (1, 5, 9, 12)),
+    ("backward", 1, 0, (12, 19, 22, 24)),
+    ("pass_on", 0, 0, (10, 13, 17, 22)),
+    ("narrow", 0, 0, (17, 18, 24, 25)),
+    ("narrow", 1, 0, (15, 24, 25, 26)),
+    ("finish", 0, 0, (22, 23, 28, 29)),
+    ("settle_on", None, 0, (19, 23, 26, 27)),
+    ("up_grads", 0, 0, (27,)),
+    ("finish", 1, 0, (23, 27, 29, 30)),
 )
-TICKS = 27
+TICKS = 31
 
 
 def column_tiles(width):

time: 95.8 us -> 96.7 us (level)
  Pallas kernels: 95 us -> 96 us
where the time goes in v6:
time: 96.7 us; the launch traced here: 96.6 us
  Pallas kernels  96 us (99%)
    pallas_call x1, Pallas kernels, local(): pl.pallas_call(functools.partial(kernel, dims), out_shape=(jax.ShapeDtype...  90.7 us
    pallas_call x1, Pallas kernels, local(): pl.pallas_call(publish, out_shape=tuple((jax.ShapeDtypeStruct(r.shape, r....  5.26 us

profile of v6, /device:TPU:0, one launch (start us, length us, event | category | flops | bytes accessed | tf_op | source)
XLA Modules:
  0.0 96.6 jit_solution(17252519437817207300)
XLA Ops:
  0.6 90.7 %shard_map.119 = (bf16[4,16,1024]{2,1,0:T(8,128)(2,1)}, bf16[4,16,1024]{2,1,0:T(8,128)(2,1)}, bf16[1024,896]{1,0:T(8,128)(2,1)}, bf16[1024,896]{1,0:T(8,128)(2,1)}, bf16[896,1024]{1,0:T(8,128)(2,1)}) custom-call(bf16[4,16,1024]{2,1,0:T(8,128)(2,1)} %bitcast.4, bf16[4,16,1024]{2,1,0:T(8,128)(2,1)} %bitcast.5, bf16[1024,896]{1,0:T(8,128)(2,1)} %gate_hbm.1, ...), custom_call_target="tpu_custom_call" | custom-call | tf_op jit(solution)/shard_map/pallas_call | solution.py:460
  91.3 5.3 %shard_map.120 = (bf16[4,16,1024]{2,1,0:T(8,128)(2,1)}, bf16[4,16,1024]{2,1,0:T(8,128)(2,1)}, bf16[1024,896]{1,0:T(8,128)(2,1)}, bf16[1024,896]{1,0:T(8,128)(2,1)}, bf16[896,1024]{1,0:T(8,128)(2,1)}) custom-call(bf16[4,16,1024]{2,1,0:T(8,128)(2,1)} %get-tuple-element.15.refs_0_, bf16[4,16,1024]{2,1,0:T(8,128)(2,1)} %get-tuple-element.16.refs_1_, ...), custom_call_target="tpu_custom_call" | custom-call | tf_op jit(solution)/shard_map/pallas_call | solution.py:510
